TPU v7x, 256 devices: a whole 4x4x8 slice. The times are simulated.
256 devices in a mesh: expert: 32 (over z, x), dp: 8 (over y, core).
Axes of the slice: x: 4, y: 4, z: 8, core: 2. Of those that a mesh axis runs over, the one named last changes fastest.
Arguments:
- tokens: bfloat16 [3072, 4096], P('expert', 'dp'), may hold values from -6 to 6
- route_weight: float32 [3072, 8], P('expert'), may hold values from 0.05 to 0.25
- route_expert: int32 [3072, 8], P('expert'), may hold values from 0 to 31, all different within a row; in each aligned block of 96 rows (0 to 95, 96 to 191, ...) at most 32 rows name the same one
- cotangent: bfloat16 [3072, 4096], P('expert', 'dp'), may hold values from -6 to 6
- gate_quant: bfloat16 [32, 4096, 1024], P('expert', None, 'dp'), may hold values from -0.09375 to 0.09375
- up_quant: bfloat16 [32, 4096, 1024], P('expert', None, 'dp'), may hold values from -0.09375 to 0.09375
- gate_scale: float32 [32, 32, 8], P('expert', None, 'dp'), may hold values from 0.5 to 2
- up_scale: float32 [32, 32, 8], P('expert', None, 'dp'), may hold values from 0.5 to 2
- down_quant: bfloat16 [32, 1024, 4096], P('expert', None, 'dp'), may hold values from -0.1875 to 0.1875
- down_scale: float32 [32, 8, 32], P('expert', None, 'dp'), may hold values from 0.5 to 2
- first_moment: float32 [32, 1024, 4096], P('expert', None, 'dp'), may hold values from -6 to 6
- second_moment: float32 [32, 1024, 4096], P('expert', None, 'dp'), may hold values from 0.5 to 8
- old_expert: int32 [32], replicated, may hold values from 0 to 31, each once
- new_holder: int32 [32], replicated, may hold values from 0 to 31, each once
Outputs:
- mixed: bfloat16 [3072, 4096], P('expert', 'dp')
- new_down: bfloat16 [32, 1024, 4096], P('expert', None, 'dp')
- new_first: float32 [32, 1024, 4096], P('expert', None, 'dp')
- new_second: float32 [32, 1024, 4096], P('expert', None, 'dp')
Inputs may be any that keep to these rules, and one draw needn't show every extreme that they name: `route_expert`: within each aligned block of 96 tokens (the tokens of one index of expert) no expert is named by more than 32 routes, a bound that some block reaches; a token names 8 different experts. `old_expert`: A permutation of the experts. `new_holder`: A permutation of the indices of expert.
All inputs are finite; a program needn't handle non-finite values.
Results may differ from a plain program's by a relative error of at most 0.0076.
Values may be sent and summed in bfloat16 or wider, within the bound.
A program may use at most 128 MiB of HBM per device.

v0:
```python
import jax
import jax.numpy as jnp
from jax import lax
from jax.sharding import PartitionSpec as P

QB = 128


beta_first = 0.9
beta_second = 0.95
adam_eps = 1e-08
learn_rate = 0.003
decay_rate = 0.1
step_count = 20


def dequantize(quant, scale):
    tiled = jnp.repeat(jnp.repeat(scale, QB, axis=0), QB, axis=1)
    return quant.astype(jnp.float32) * tiled


def adam_step(master, grad, first, second):
    first_new = beta_first * first + (1.0 - beta_first) * grad
    second_new = beta_second * second + (1.0 - beta_second) * grad * grad
    fix_first = 1.0 - beta_first**step_count
    fix_second = 1.0 - beta_second**step_count
    update = first_new / fix_first / (jnp.sqrt(second_new / fix_second) + adam_eps)
    fresh = (master - learn_rate * (update + decay_rate * master)).astype(jnp.bfloat16)
    return (fresh, first_new, second_new)


def holder_tables(old_expert, new_holder):
    number = old_expert.shape[0]
    labels = jnp.arange(number, dtype=jnp.int32)
    holds = (old_expert[:, None] == labels[None, :]).astype(jnp.int32)
    old_device = jnp.sum(holds * labels[:, None], axis=0)
    new_device = jnp.sum(holds * new_holder[:, None], axis=0)
    takes = (new_holder[:, None] == labels[None, :]).astype(jnp.int32)
    giver = jnp.sum(takes * labels[:, None], axis=0)
    return (old_device, new_device, giver)


def pack_rows(arrays, number):
    lines = []
    for array_item in arrays:
        line = array_item.reshape(-1)
        lines.append(line.reshape(number, -1))
    return jnp.concatenate(lines, axis=1)


def unpack_rows(packed, arrays):
    number = packed.shape[0]
    result = []
    offset = 0
    for array_item in arrays:
        span_cols = -(-array_item.size // number)
        block_rows = packed[:, offset : offset + span_cols]
        result.append(block_rows.reshape(-1).reshape(array_item.shape))
        offset = offset + span_cols
    return tuple(result)


def move_weights(arrays, giver):
    packed = pack_rows(arrays, giver.shape[0])
    spread = lax.all_to_all(packed, "expert", split_axis=0, concat_axis=0, tiled=True)
    settled = lax.all_to_all(
        jnp.take(spread, giver, axis=0), "expert", split_axis=0, concat_axis=0, tiled=True
    )
    return unpack_rows(settled, arrays)


def move_state(arrays, giver):
    packed = pack_rows(arrays, giver.shape[0])
    spread = lax.all_to_all(packed, "expert", split_axis=0, concat_axis=0, tiled=True)
    settled = lax.all_to_all(
        jnp.take(spread, giver, axis=0), "expert", split_axis=0, concat_axis=0, tiled=True
    )
    return unpack_rows(settled, arrays)


def plan_slots(route_expert, target_of, number, capacity):
    route_total = route_expert.shape[0] * route_expert.shape[1]
    flat_expert = route_expert.reshape(-1)
    labels = jnp.arange(number, dtype=jnp.int32)
    pick = (flat_expert[:, None] == labels[None, :]).astype(jnp.int32)
    target = jnp.sum(pick * target_of[None, :], axis=1)
    onehot = (target[:, None] == labels[None, :]).astype(jnp.int32)
    earlier = jnp.cumsum(onehot, axis=0) - onehot
    slot_index = jnp.sum(earlier * onehot, axis=1)
    route_place = target * capacity + slot_index
    slot_route = (
        jnp.full((number * capacity,), -1, jnp.int32)
        .at[route_place]
        .set(jnp.arange(route_total, dtype=jnp.int32))
    )
    return (route_place, slot_route)


def per_device(
    tokens,
    route_weight,
    route_expert,
    cotangent,
    gate_quant,
    up_quant,
    gate_scale,
    up_scale,
    down_quant,
    down_scale,
    first_moment,
    second_moment,
    old_expert,
    new_holder,
):
    number = lax.axis_size("expert")
    tok_rows, top_count = route_expert.shape
    model_width = gate_quant.shape[1]
    column_width = cotangent.shape[1]
    capacity = min(tok_rows, tok_rows * top_count // number * 4 // 3)
    old_device, new_device, giver = holder_tables(old_expert, new_holder)
    gate_quant, up_quant, down_quant = move_weights((gate_quant, up_quant, down_quant), giver)
    gate_scale, up_scale, down_scale, first_moment, second_moment = move_state(
        (gate_scale, up_scale, down_scale, first_moment, second_moment), giver
    )
    route_place, slot_route = plan_slots(route_expert, new_device, number, capacity)
    live_rows = slot_route >= 0
    safe_route = jnp.maximum(slot_route, 0)
    token_ids = safe_route // top_count
    weight_rows = jnp.where(
        live_rows, jnp.take(route_weight.reshape(-1), safe_route), jnp.float32(0.0)
    )
    back_rows = (
        weight_rows[:, None] * jnp.take(cotangent, token_ids, axis=0).astype(jnp.float32)
    ).astype(jnp.bfloat16)
    back_send = back_rows.reshape(number, capacity, column_width)
    whole_tokens = lax.all_gather(tokens, "dp", axis=1, tiled=True)
    sent_rows = jnp.take(whole_tokens, token_ids, axis=0).reshape(number, capacity, model_width)
    arrived, back_in = (
        lax.all_to_all(sent_rows, "expert", split_axis=0, concat_axis=0, tiled=True),
        lax.all_to_all(back_send, "expert", split_axis=0, concat_axis=0, tiled=True),
    )
    rows_in = arrived.reshape(-1, model_width)
    back_in = back_in.reshape(-1, column_width)
    gate_w = dequantize(gate_quant[0], gate_scale[0]).astype(jnp.bfloat16)
    up_w = dequantize(up_quant[0], up_scale[0]).astype(jnp.bfloat16)
    master = dequantize(down_quant[0], down_scale[0])
    down_w = master.astype(jnp.bfloat16)
    gate_val = jnp.dot(rows_in, gate_w, preferred_element_type=jnp.float32)
    up_val = jnp.dot(rows_in, up_w, preferred_element_type=jnp.float32)
    hidden_part = (jax.nn.silu(gate_val) * up_val).astype(jnp.bfloat16)
    hidden_full = lax.all_gather(hidden_part, "dp", axis=1, tiled=True)
    out_total = jnp.dot(hidden_full, down_w, preferred_element_type=jnp.float32)
    grad_total = lax.dot_general(
        hidden_full, back_in, (((0,), (0,)), ((), ())), preferred_element_type=jnp.float32
    )
    out_rows = out_total.astype(jnp.bfloat16).reshape(number, capacity, column_width)
    returned = lax.all_to_all(out_rows, "expert", split_axis=0, concat_axis=0, tiled=True).reshape(
        -1, column_width
    )
    picked = (
        jnp.take(returned, route_place, axis=0)
        .reshape(tok_rows, top_count, column_width)
        .astype(jnp.float32)
    )
    mixed = jnp.sum(picked * route_weight[:, :, None], axis=1).astype(jnp.bfloat16)
    fresh, first_new, second_new = adam_step(master, grad_total, first_moment[0], second_moment[0])
    fresh = fresh[None]
    first_new = first_new[None]
    second_new = second_new[None]
    return (mixed, fresh, first_new, second_new)


def solution(mesh):
    in_specs = (
        P("expert", "dp"),
        P("expert", None),
        P("expert", None),
        P("expert", "dp"),
        P("expert", None, "dp"),
        P("expert", None, "dp"),
        P("expert", None, "dp"),
        P("expert", None, "dp"),
        P("expert", None, "dp"),
        P("expert", None, "dp"),
        P("expert", None, "dp"),
        P("expert", None, "dp"),
        P(),
        P(),
    )
    out_specs = (
        P("expert", "dp"),
        P("expert", None, "dp"),
        P("expert", None, "dp"),
        P("expert", None, "dp"),
    )
    return jax.shard_map(
        per_device, mesh=mesh, in_specs=in_specs, out_specs=out_specs, check_vma=False
    )
```

profile of v0, /device:TPU:1, one launch (start us, length us, event | category | flops | bytes accessed | tf_op | source)
XLA Modules:
  0.0 697.2 jit_solution(656383670032208674)
XLA Ops:
  18.5 5.4 reshape.303
  23.9 12.0 %all-to-all-start.1 = ((bf16[32,2,24576]{2,1,0:T(2,128)(2,1)}), bf16[32,2,24576]{2,1,0:T(2,128)(2,1)S(1)}, u32[]{:S(2)}, u32[]{:S(2)}) async-start(bf16[32,2,24576]{2,1,0:T(2,128)(2,1)} %reshape.303), calls=%async_computation.1 | async-start | bytes 6291456 | tf_op jit(solution)/shard_map/all_to_all | solution.py:65
  45.9 9.3 %dynamic-update-slice.3 = f32[32,32771]{1,0:T(8,128)} dynamic-update-slice(f32[32,32771]{1,0:T(8,128)} %dynamic-update-slice.2, f32[32,16384]{1,0:T(8,128)} %reshape_reshape.30, s32[]{} %constant.150, s32[]{} %constant.153) | dynamic-update-slice | bytes 4194308
  55.1 8.7 %dynamic-update-slice.4 = f32[32,32771]{1,0:T(8,128)} dynamic-update-slice(f32[32,32771]{1,0:T(8,128)} %dynamic-update-slice.3, f32[32,16384]{1,0:T(8,128)} %reshape_reshape.31, s32[]{} %constant.150, s32[]{} %constant.154) | dynamic-update-slice | bytes 4194308 | tf_op jit(solution)/shard_map/concatenate | solution.py:48
  63.8 9.8 %all_to_all.43 = f32[32,1,32771]{2,1,0:T(1,128)} reshape(f32[32,32771]{1,0:T(8,128)} %dynamic-update-slice.4) | data formatting | bytes 8389376 | tf_op jit(solution)/shard_map/all_to_all | solution.py:74
  73.8 32.5 %all-to-all-done.1 = bf16[32,2,24576]{2,1,0:T(2,128)(2,1)S(1)} async-done(((bf16[32,2,24576]{2,1,0:T(2,128)(2,1)}), bf16[32,2,24576]{2,1,0:T(2,128)(2,1)S(1)}, u32[]{:S(2)}, u32[]{:S(2)}) %all-to-all-start.1) | async-done | bytes 3145760 | tf_op jit(solution)/shard_map/all_to_all | solution.py:65
  106.2 8.3 %all-to-all-start.3 = ((f32[32,1,32771]{2,1,0:T(1,128)}), f32[32,1,32771]{2,1,0:T(1,128)}, u32[]{:S(2)}, u32[]{:S(2)}) async-start(f32[32,1,32771]{2,1,0:T(1,128)} %all_to_all.43), calls=%async_computation.3 | async-start | bytes 8421376 | tf_op jit(solution)/shard_map/all_to_all | solution.py:74
  114.5 12.4 %reshape.304 = bf16[32,1,49152]{2,1,0:T(2,128)(2,1)} reshape(bf16[32,2,24576]{2,1,0:T(2,128)(2,1)S(1)} %all-to-all-done.1) | data formatting | bytes 6291456
  127.0 6.2 copy.83
  143.5 5.4 reshape.305
  148.9 58.3 %all-to-all-done.3 = f32[32,1,32771]{2,1,0:T(1,128)} async-done(((f32[32,1,32771]{2,1,0:T(1,128)}), f32[32,1,32771]{2,1,0:T(1,128)}, u32[]{:S(2)}, u32[]{:S(2)}) %all-to-all-start.3) | async-done | bytes 4194720 | tf_op jit(solution)/shard_map/all_to_all | solution.py:74
  207.2 9.5 %all-to-all-start.2 = ((bf16[32,2,24576]{2,1,0:T(2,128)(2,1)}), bf16[32,2,24576]{2,1,0:T(2,128)(2,1)}, u32[]{:S(2)}, u32[]{:S(2)}) async-start(bf16[32,2,24576]{2,1,0:T(2,128)(2,1)} %reshape.305), calls=%async_computation.2 | async-start | bytes 6291456 | tf_op jit(solution)/shard_map/all_to_all | solution.py:66
  221.0 7.6 %gather_fusion.2 = f32[32,32771]{1,0:T(8,128)} fusion(f32[32,32771]{1,0:T(8,128)} %bitcast.77, s32[1024]{0:T(1024)S(1)} %pad_clamp_fusion.1), kind=kCustom, calls=%fused_computation.2 | custom fusion | bytes 8389504 | tf_op jit(solution)/shard_map/jit(_take)/gather | solution.py:76
  231.2 6.3 copy.60
  237.5 49.4 %all-to-all-done.2 = bf16[32,2,24576]{2,1,0:T(2,128)(2,1)} async-done(((bf16[32,2,24576]{2,1,0:T(2,128)(2,1)}), bf16[32,2,24576]{2,1,0:T(2,128)(2,1)}, u32[]{:S(2)}, u32[]{:S(2)}) %all-to-all-start.2) | async-done | bytes 3145760 | tf_op jit(solution)/shard_map/all_to_all | solution.py:66
  286.9 8.1 %all-to-all-start.4 = ((f32[32,1,32771]{2,1,0:T(1,128)}), f32[32,1,32771]{2,1,0:T(1,128)}, u32[]{:S(2)}, u32[]{:S(2)}) async-start(f32[32,1,32771]{2,1,0:T(1,128)} %copy.60), calls=%async_computation.4 | async-start | bytes 8421376 | tf_op jit(solution)/shard_map/all_to_all | solution.py:75
  301.0 15.2 %all_gather.6 = bf16[96,4096]{1,0:T(8,128)(2,1)S(1)} all-gather(bf16[96,512]{1,0:T(8,128)(2,1)S(1)} %copy-done.7), channel_id=1, replica_groups=mesh['expert'=32,'dp'=8] {'dp'}, dimensions={1}, use_global_device_ids=true | all-gather | bytes 884736 | tf_op jit(solution)/shard_map/all_gather | solution.py:136
  316.2 7.8 %gather_fusion = bf16[1024,4096]{1,0:T(8,128)(2,1)} fusion(bf16[96,4096]{1,0:T(8,128)(2,1)S(1)} %all_gather.6, s32[1024]{0:T(1024)S(1)} %get-tuple-element.17), kind=kCustom, calls=%fused_computation | custom fusion | bytes 16781312 | tf_op jit(solution)/shard_map/jit(_take)/gather | solution.py:137
  324.0 7.4 %broadcast_select_fusion = bf16[32,32,4096]{2,1,0:T(8,128)(2,1)} fusion(bf16[32,32,4096]{2,1,0:T(8,128)(2,1)} %bitcast.80, pred[32,32]{1,0:T(8,128)(4,1)S(1)} %broadcast_in_dim.103), kind=kLoop, calls=%fused_computation.7 | loop fusion | flops 4194304 | bytes 16778240 | tf_op jit(solution)/shard_map/jit(_take)/select_n | solution.py:137
  331.4 56.2 %all-to-all-done.4 = f32[32,1,32771]{2,1,0:T(1,128)} async-done(((f32[32,1,32771]{2,1,0:T(1,128)}), f32[32,1,32771]{2,1,0:T(1,128)}, u32[]{:S(2)}, u32[]{:S(2)}) %all-to-all-start.4) | async-done | bytes 4194720 | tf_op jit(solution)/shard_map/all_to_all | solution.py:75
  387.6 9.1 %all-to-all-start = ((bf16[32,32,4096]{2,1,0:T(8,128)(2,1)}), bf16[32,32,4096]{2,1,0:T(8,128)(2,1)}, u32[]{:S(2)}, u32[]{:S(2)}) async-start(bf16[32,32,4096]{2,1,0:T(8,128)(2,1)} %broadcast_select_fusion), calls=%async_computation | async-start | bytes 16777216 | tf_op jit(solution)/shard_map/all_to_all | solution.py:139
  406.9 18.9 %reshape.306 = bf16[32,1,49152]{2,1,0:T(2,128)(2,1)} reshape(bf16[32,2,24576]{2,1,0:T(2,128)(2,1)} %all-to-all-done.2) | data formatting | bytes 6291456
  425.8 6.2 copy.82
  441.8 142.5 %all-to-all-done = bf16[32,32,4096]{2,1,0:T(8,128)(2,1)} async-done(((bf16[32,32,4096]{2,1,0:T(8,128)(2,1)}), bf16[32,32,4096]{2,1,0:T(8,128)(2,1)}, u32[]{:S(2)}, u32[]{:S(2)}) %all-to-all-start) | async-done | bytes 8388640 | tf_op jit(solution)/shard_map/all_to_all | solution.py:139
  584.3 15.6 %all-to-all-start.6 = ((bf16[32,32,512]{2,1,0:T(8,128)(2,1)}), bf16[32,32,512]{2,1,0:T(8,128)(2,1)}, u32[]{:S(2)}, u32[]{:S(2)}) async-start(bf16[32,32,512]{2,1,0:T(8,128)(2,1)} %multiply_convert_fusion), calls=%async_computation.6 | async-start | bytes 2097152 | tf_op jit(solution)/shard_map/all_to_all | solution.py:140
  600.2 6.0 fusion.15
  606.2 6.4 fusion.1
  616.0 28.9 %all-gather.2.cloned.1.call-done = bf16[1024,1024]{1,0:T(8,128)(2,1)} async-done(((bf16[1024,128]{1,0:T(8,128)(2,1)}), bf16[1024,1024]{1,0:T(8,128)(2,1)}) %all-gather.2.cloned.1.call-update) | async-done | bytes 2097168 | tf_op jit(solution)/shard_map/all_gather | solution.py:151
  649.8 9.5 %all-to-all-start.5 = ((bf16[32,32,512]{2,1,0:T(8,128)(2,1)}), bf16[32,32,512]{2,1,0:T(8,128)(2,1)S(1)}, u32[]{:S(2)}, u32[]{:S(2)}) async-start(bf16[32,32,512]{2,1,0:T(8,128)(2,1)} %bitcast.12), calls=%async_computation.5 | async-start | bytes 2097152 | tf_op jit(solution)/shard_map/all_to_all | solution.py:157
  659.3 4.7 slice_multiply_fusion
  668.3 9.3 %fusion.5 = (f32[1,1024,512]{2,1,0:T(8,128)}, bf16[1,1024,512]{2,1,0:T(8,128)(2,1)}, f32[1,1024,512]{2,1,0:T(8,128)}) fusion(f32[1024,512]{1,0:T(8,128)} %mul.146, f32[1024,512]{1,0:T(8,128)} %mul.139, f32[1024,512]{1,0:T(8,128)} %copy-done.3, f32[128,8,4,128]{3,2,1,0:T(4,128)} %bitcast.87, bf16[1024,1024]{1,0:T(8,128)(2,1)} %all-gather.2.cloned.1.call-done, ...), kind=kOutput, calls=%fused_computation.34 | convolution fusion | flops 1081606144 | bytes 16777216 | tf_op jit(solution)/shard_map/dot_general | solution.py:153
  677.6 8.6 %all-to-all-done.5 = bf16[32,32,512]{2,1,0:T(8,128)(2,1)S(1)} async-done(((bf16[32,32,512]{2,1,0:T(8,128)(2,1)}), bf16[32,32,512]{2,1,0:T(8,128)(2,1)S(1)}, u32[]{:S(2)}, u32[]{:S(2)}) %all-to-all-start.5) | async-done | bytes 1048608 | tf_op jit(solution)/shard_map/all_to_all | solution.py:157
  (100 shorter events, 81.0 us)
Async XLA Ops:
  7.2 394.4 %copy-start = (bf16[96,512]{1,0:T(8,128)(2,1)S(1)}, bf16[96,512]{1,0:T(8,128)(2,1)}, u32[]{:S(2)}) copy-start(bf16[96,512]{1,0:T(8,128)(2,1)} %param.17) | copy-start | bytes 294916
  7.2 2.5 copy-start.4
  7.2 3.7 copy-start.5
  23.9 12.0 %copy-start.11 = (f32[1,32,1]{1,2,0:T(1,128)S(1)}, f32[1,32,1]{1,2,0:T(1,128)}, u32[]{:S(2)}) copy-start(f32[1,32,1]{1,2,0:T(1,128)} %param.20) | copy-start | bytes 388
  23.9 12.1 %copy-start.12 = (f32[1,32,1]{1,2,0:T(1,128)S(1)}, f32[1,32,1]{1,2,0:T(1,128)}, u32[]{:S(2)}) copy-start(f32[1,32,1]{1,2,0:T(1,128)} %param.21) | copy-start | bytes 388
  23.9 12.2 %copy-start.10 = (f32[1,8,4]{1,2,0:T(4,128)S(1)}, f32[1,8,4]{1,2,0:T(4,128)}, u32[]{:S(2)}) copy-start(f32[1,8,4]{1,2,0:T(4,128)} %param.23) | copy-start | bytes 388
  23.9 82.3 %all-to-all-start.1 = ((bf16[32,2,24576]{2,1,0:T(2,128)(2,1)}), bf16[32,2,24576]{2,1,0:T(2,128)(2,1)S(1)}, u32[]{:S(2)}, u32[]{:S(2)}) async-start(bf16[32,2,24576]{2,1,0:T(2,128)(2,1)} %reshape.303), calls=%async_computation.1 | async-start | bytes 6291456 | tf_op jit(solution)/shard_map/all_to_all | solution.py:65
  63.8 9.8 %copy-start.13 = (s32[32]{0:T(128)S(1)}, s32[32]{0:T(128)}, u32[]{:S(2)}) copy-start(s32[32]{0:T(128)} %param.27) | copy-start | bytes 388
  63.8 9.8 %copy-start.14 = (s32[32]{0:T(128)S(1)}, s32[32]{0:T(128)}, u32[]{:S(2)}) copy-start(s32[32]{0:T(128)} %param.26) | copy-start | bytes 388
  106.2 100.9 %all-to-all-start.3 = ((f32[32,1,32771]{2,1,0:T(1,128)}), f32[32,1,32771]{2,1,0:T(1,128)}, u32[]{:S(2)}, u32[]{:S(2)}) async-start(f32[32,1,32771]{2,1,0:T(1,128)} %all_to_all.43), calls=%async_computation.3 | async-start | bytes 8421376 | tf_op jit(solution)/shard_map/all_to_all | solution.py:74
  207.2 79.8 %all-to-all-start.2 = ((bf16[32,2,24576]{2,1,0:T(2,128)(2,1)}), bf16[32,2,24576]{2,1,0:T(2,128)(2,1)}, u32[]{:S(2)}, u32[]{:S(2)}) async-start(bf16[32,2,24576]{2,1,0:T(2,128)(2,1)} %reshape.305), calls=%async_computation.2 | async-start | bytes 6291456 | tf_op jit(solution)/shard_map/all_to_all | solution.py:66
  237.5 57.5 %copy-start.8 = (s32[96,8]{0,1:T(8,128)S(1)}, s32[96,8]{0,1:T(8,128)}, u32[]{:S(2)}) copy-start(s32[96,8]{0,1:T(8,128)} %param.16) | copy-start | bytes 9220
  237.5 63.5 %copy-start.7 = (bf16[96,512]{1,0:T(8,128)(2,1)S(1)}, bf16[96,512]{1,0:T(8,128)(2,1)}, u32[]{:S(2)}) copy-start(bf16[96,512]{1,0:T(8,128)(2,1)} %param.14) | copy-start | bytes 294916
  286.9 100.7 %all-to-all-start.4 = ((f32[32,1,32771]{2,1,0:T(1,128)}), f32[32,1,32771]{2,1,0:T(1,128)}, u32[]{:S(2)}, u32[]{:S(2)}) async-start(f32[32,1,32771]{2,1,0:T(1,128)} %copy.60), calls=%async_computation.4 | async-start | bytes 8421376 | tf_op jit(solution)/shard_map/all_to_all | solution.py:75
  331.4 65.4 %copy-start.9 = (f32[96,8]{0,1:T(8,128)S(1)}, f32[96,8]{0,1:T(8,128)}, u32[]{:S(2)}) copy-start(f32[96,8]{0,1:T(8,128)} %param.15) | copy-start | bytes 9220
  387.6 196.7 %all-to-all-start = ((bf16[32,32,4096]{2,1,0:T(8,128)(2,1)}), bf16[32,32,4096]{2,1,0:T(8,128)(2,1)}, u32[]{:S(2)}, u32[]{:S(2)}) async-start(bf16[32,32,4096]{2,1,0:T(8,128)(2,1)} %broadcast_select_fusion), calls=%async_computation | async-start | bytes 16777216 | tf_op jit(solution)/shard_map/all_to_all | solution.py:139
  434.5 2.6 copy-start.1
  584.3 65.5 %all-to-all-start.6 = ((bf16[32,32,512]{2,1,0:T(8,128)(2,1)}), bf16[32,32,512]{2,1,0:T(8,128)(2,1)}, u32[]{:S(2)}, u32[]{:S(2)}) async-start(bf16[32,32,512]{2,1,0:T(8,128)(2,1)} %multiply_convert_fusion), calls=%async_computation.6 | async-start | bytes 2097152 | tf_op jit(solution)/shard_map/all_to_all | solution.py:140
  599.9 45.0 %all-gather.2.cloned.1.call-start = ((), (), s32[]{:S(2)}) async-start(), calls=%async_computation.7 | async-start | bytes 2359296 | tf_op jit(solution)/shard_map/all_gather | solution.py:151
  600.2 6.0 copy-start.6
  615.9 33.9 %copy-start.3 = (f32[1024,512]{1,0:T(8,128)}, f32[1024,512]{1,0:T(8,128)S(1)}, u32[]{:S(2)}) copy-start(f32[1024,512]{1,0:T(8,128)S(1)} %reshape.234) | copy-start | bytes 6291460
  644.9 2.6 copy-start.15
  646.2 1.3 copy-start.2
  649.8 36.4 %all-to-all-start.5 = ((bf16[32,32,512]{2,1,0:T(8,128)(2,1)}), bf16[32,32,512]{2,1,0:T(8,128)(2,1)S(1)}, u32[]{:S(2)}, u32[]{:S(2)}) async-start(bf16[32,32,512]{2,1,0:T(8,128)(2,1)} %bitcast.12), calls=%async_computation.5 | async-start | bytes 2097152 | tf_op jit(solution)/shard_map/all_to_all | solution.py:157
Sparse Core Ops, SparseCore 0:
  612.8 32.0 all-gather.1
where the time goes:
time: 706 us; the launch traced here: 697 us
  waiting for transfers between devices  376 us (53%)
  local copies, waits for them, and re-layouts  160 us (23%)
  starting transfers between devices  72.3 us (10%)
  other arithmetic  34.7 us (5%)
  matrix products  24 us (3%)
  blocking collectives  15.2 us (2%)
  between operations  14.6 us (2%)
    all_to_all x1, waiting for transfers between devices, per_device(): lax.all_to_all(sent_rows, 'expert', split_axis=0, concat_axis=0, tiled=True)  143 us
    unnamed x47, local copies, waits for them, and re-layouts  76.8 us
    all_to_all x1, waiting for transfers between devices, move_state(): lax.all_to_all(packed, 'expert', split_axis=0, concat_axis=0, tiled=True)  58.3 us
    all_to_all x1, waiting for transfers between devices, move_state(): lax.all_to_all(jnp.take(spread, giver, axis=0), 'expert', split_axis=0, c...  56.2 us
    all_to_all x1, waiting for transfers between devices, move_weights(): lax.all_to_all(jnp.take(spread, giver, axis=0), 'expert', split_axis=0, c...  49.4 us
    all_to_all x1, waiting for transfers between devices, move_weights(): lax.all_to_all(packed, 'expert', split_axis=0, concat_axis=0, tiled=True)  32.5 us
    all_gather x1, waiting for transfers between devices, per_device(): hidden_full = lax.all_gather(hidden_part, 'dp', axis=1, tiled=True)  28.9 us
    all_to_all x1, starting transfers between devices, per_device(): lax.all_to_all(back_send, 'expert', split_axis=0, concat_axis=0, tiled=True)  15.6 us
  transfers between devices with their start and end apart: 8, of which 7 were waited for; matrix products, arithmetic and copies ran while one was open for 27% of the time, Pallas kernels for 0%

commit v1 on v0

v1 whole, which is shorter than its diff:
```python
import jax
import jax.numpy as jnp
from jax import lax
from jax.experimental import pallas as pl
from jax.experimental.pallas import tpu as pltpu
from jax.sharding import PartitionSpec as P

QB = 128
BF = jnp.bfloat16
F32 = jnp.float32

beta_first = 0.9
beta_second = 0.95
adam_eps = 1e-08
learn_rate = 0.003
decay_rate = 0.1
step_count = 20
fix_first = 1.0 - beta_first**step_count
fix_second = 1.0 - beta_second**step_count

VMEM_LIMIT = 48 * 1024 * 1024


def split_bits(value):
    high = lax.reduce_precision(value, 8, 7)
    rest = value - high
    middle = lax.reduce_precision(rest, 8, 7)
    low = rest - middle
    return high.astype(BF), middle.astype(BF), low.astype(BF)


def ranks(mask):
    count = mask.shape[-1]
    i = jnp.arange(count)
    earlier = (i[:, None] < i[None, :]).astype(BF)
    position = jnp.dot(mask.astype(BF), earlier, preferred_element_type=F32)
    return jnp.where(mask > 0, position, -1.0)


def compact_kernel(rank_ref, table_ref, out_ref):
    blocks, rows, _ = table_ref.shape
    slots = out_ref.shape[0] // blocks
    for s in range(blocks):
        place = lax.broadcasted_iota(jnp.int32, (slots, rows), 0).astype(F32)
        pick = (rank_ref[s : s + 1, :] == place).astype(BF)
        picked = jnp.dot(pick, table_ref[s], preferred_element_type=F32)
        out_ref[s * slots : (s + 1) * slots, :] = picked.astype(BF)


def compact(rank, table, slots, width):
    blocks, rows, _ = table.shape
    return pl.pallas_call(
        compact_kernel,
        grid=(1,),
        in_specs=[
            pl.BlockSpec((blocks, rows), lambda i: (0, 0)),
            pl.BlockSpec((blocks, rows, width), lambda i: (0, 0, 0)),
        ],
        out_specs=pl.BlockSpec((blocks * slots, width), lambda i: (0, 0)),
        out_shape=jax.ShapeDtypeStruct((blocks * slots, width), BF),
        compiler_params=pltpu.CompilerParams(vmem_limit_bytes=VMEM_LIMIT),
        cost_estimate=pl.CostEstimate(
            flops=2 * blocks * slots * rows * width, bytes_accessed=4 << 20, transcendentals=0
        ),
        name="compact",
    )(rank, table)


def back_kernel(rank_ref, weight_ref, table_ref, out_ref):
    blocks, rows, _ = table_ref.shape
    slots = out_ref.shape[0] // blocks
    for s in range(blocks):
        place = lax.broadcasted_iota(jnp.int32, (slots, rows), 0).astype(F32)
        hit = rank_ref[s : s + 1, :] == place
        weight = jnp.sum(jnp.where(hit, weight_ref[s : s + 1, :], 0.0), axis=1, keepdims=True)
        picked = jnp.dot(hit.astype(BF), table_ref[s], preferred_element_type=F32)
        out_ref[s * slots : (s + 1) * slots, :] = (weight * picked).astype(BF)


def weighted_compact(rank, weight, table, slots, width):
    blocks, rows, _ = table.shape
    return pl.pallas_call(
        back_kernel,
        grid=(1,),
        in_specs=[
            pl.BlockSpec((blocks, rows), lambda i: (0, 0)),
            pl.BlockSpec((blocks, rows), lambda i: (0, 0)),
            pl.BlockSpec((blocks, rows, width), lambda i: (0, 0, 0)),
        ],
        out_specs=pl.BlockSpec((blocks * slots, width), lambda i: (0, 0)),
        out_shape=jax.ShapeDtypeStruct((blocks * slots, width), BF),
        compiler_params=pltpu.CompilerParams(vmem_limit_bytes=VMEM_LIMIT),
        cost_estimate=pl.CostEstimate(
            flops=2 * blocks * slots * rows * width, bytes_accessed=4 << 20, transcendentals=0
        ),
        name="back_rows",
    )(rank, weight, table)


def gate_up_kernel(gs_ref, us_ref, x_ref, gq_ref, uq_ref, out_ref, acc_ref):
    k = pl.program_id(0)
    depth, hidden = gq_ref.shape
    per = depth // QB

    @pl.when(k == 0)
    def _():
        acc_ref[...] = jnp.zeros_like(acc_ref)

    gates, ups = [], []
    for j in range(per):
        rows = slice(j * QB, (j + 1) * QB)
        gates.append((gq_ref[rows, :].astype(F32) * gs_ref[k * per + j]).astype(BF))
        ups.append((uq_ref[rows, :].astype(F32) * us_ref[k * per + j]).astype(BF))
    weights = jnp.concatenate(
        [jnp.concatenate(gates, axis=0), jnp.concatenate(ups, axis=0)], axis=1
    )
    acc_ref[...] += jnp.dot(x_ref[0], weights, preferred_element_type=F32)

    @pl.when(k == pl.num_programs(0) - 1)
    def _():
        gate = acc_ref[:, :hidden]
        up = acc_ref[:, hidden:]
        out_ref[...] = (gate / (1.0 + jnp.exp(-gate)) * up).astype(BF)


def gate_up(rows_in, gate_quant, up_quant, gate_scale, up_scale):
    parts, rows, depth = rows_in.shape
    hidden = gate_quant.shape[1]
    return pl.pallas_call(
        gate_up_kernel,
        grid=(parts,),
        in_specs=[
            pl.BlockSpec(memory_space=pltpu.SMEM),
            pl.BlockSpec(memory_space=pltpu.SMEM),
            pl.BlockSpec((1, rows, depth), lambda k: (k, 0, 0)),
            pl.BlockSpec((depth, hidden), lambda k: (k, 0)),
            pl.BlockSpec((depth, hidden), lambda k: (k, 0)),
        ],
        out_specs=pl.BlockSpec((rows, hidden), lambda k: (0, 0)),
        out_shape=jax.ShapeDtypeStruct((rows, hidden), BF),
        scratch_shapes=[pltpu.VMEM((rows, 2 * hidden), F32)],
        compiler_params=pltpu.CompilerParams(vmem_limit_bytes=VMEM_LIMIT),
        cost_estimate=pl.CostEstimate(
            flops=4 * parts * rows * depth * hidden, bytes_accessed=11 << 20, transcendentals=0
        ),
        name="gate_up",
    )(gate_scale, up_scale, rows_in, gate_quant, up_quant)


def master_rows(quant, scale_ref, tile_row):
    parts = []
    for c in range(quant.shape[1] // QB):
        parts.append(quant[:, c * QB : (c + 1) * QB].astype(F32) * scale_ref[tile_row, c])
    return jnp.concatenate(parts, axis=1)


def down_kernel(scale_ref, hidden_ref, quant_ref, out_ref, acc_ref):
    k = pl.program_id(0)
    pieces, _, piece_rows, width = quant_ref.shape

    @pl.when(k == 0)
    def _():
        acc_ref[...] = jnp.zeros_like(acc_ref)

    quant = quant_ref[...].reshape(pieces * piece_rows, width)
    down_w = master_rows(quant, scale_ref, k).astype(BF)
    acc_ref[...] += jnp.dot(hidden_ref[0], down_w, preferred_element_type=F32)

    @pl.when(k == pl.num_programs(0) - 1)
    def _():
        out_ref[...] = acc_ref[...].astype(BF)


def down(hidden, state, scale):
    parts, rows, part_hidden = hidden.shape
    number, _, piece_rows, width = state.shape
    pieces = number // parts
    return pl.pallas_call(
        down_kernel,
        grid=(parts,),
        in_specs=[
            pl.BlockSpec(memory_space=pltpu.SMEM),
            pl.BlockSpec((1, rows, part_hidden), lambda k: (k, 0, 0)),
            pl.BlockSpec((pieces, 1, piece_rows, width), lambda k: (k, 2, 0, 0)),
        ],
        out_specs=pl.BlockSpec((rows, width), lambda k: (0, 0)),
        out_shape=jax.ShapeDtypeStruct((rows, width), BF),
        scratch_shapes=[pltpu.VMEM((rows, width), F32)],
        compiler_params=pltpu.CompilerParams(vmem_limit_bytes=VMEM_LIMIT),
        cost_estimate=pl.CostEstimate(
            flops=2 * parts * rows * part_hidden * width, bytes_accessed=4 << 20, transcendentals=0
        ),
        name="down",
    )(scale, hidden, state)


def adam_kernel(scale_ref, hidden_ref, back_ref, state_ref, down_ref, first_ref, second_ref):
    k = pl.program_id(0)
    pieces, _, piece_rows, width = state_ref.shape
    rows = pieces * piece_rows
    grad = lax.dot_general(
        hidden_ref[0], back_ref[...], (((0,), (0,)), ((), ())), preferred_element_type=F32
    )
    first = state_ref[:, 0].reshape(rows, width).astype(F32)
    second = state_ref[:, 1].reshape(rows, width).astype(F32)
    master = master_rows(state_ref[:, 2].reshape(rows, width), scale_ref, k)
    first_new = beta_first * first + (1.0 - beta_first) * grad
    second_new = beta_second * second + (1.0 - beta_second) * grad * grad
    update = first_new / fix_first / (jnp.sqrt(second_new / fix_second) + adam_eps)
    down_ref[0] = (master - learn_rate * (update + decay_rate * master)).astype(BF)
    first_ref[0] = first_new
    second_ref[0] = second_new


def grad_adam(hidden, back, state, scale):
    parts, rows, part_hidden = hidden.shape
    number, kinds, piece_rows, width = state.shape
    pieces = number // parts
    total = number * piece_rows
    block = pl.BlockSpec((1, part_hidden, width), lambda k: (0, k, 0))
    return pl.pallas_call(
        adam_kernel,
        grid=(parts,),
        in_specs=[
            pl.BlockSpec(memory_space=pltpu.SMEM),
            pl.BlockSpec((1, rows, part_hidden), lambda k: (k, 0, 0)),
            pl.BlockSpec((rows, width), lambda k: (0, 0)),
            pl.BlockSpec((pieces, kinds, piece_rows, width), lambda k: (k, 0, 0, 0)),
        ],
        out_specs=[block, block, block],
        out_shape=[
            jax.ShapeDtypeStruct((1, total, width), BF),
            jax.ShapeDtypeStruct((1, total, width), F32),
            jax.ShapeDtypeStruct((1, total, width), F32),
        ],
        compiler_params=pltpu.CompilerParams(vmem_limit_bytes=VMEM_LIMIT),
        cost_estimate=pl.CostEstimate(
            flops=2 * parts * rows * part_hidden * width, bytes_accessed=11 << 20, transcendentals=0
        ),
        name="grad_adam",
    )(scale, hidden, back, state)


def mix_kernel(slots, rank_ref, weight_ref, rows_ref, out_ref):
    number = rank_ref.shape[1]
    total = number * slots
    holder = lax.broadcasted_iota(jnp.int32, (number, total), 0)
    column = lax.broadcasted_iota(jnp.int32, (number, total), 1)
    spread = (column // slots == holder).astype(BF)
    place = lax.broadcasted_iota(jnp.int32, (rank_ref.shape[0], total), 1) % slots
    rank = jnp.dot(rank_ref[...].astype(BF), spread, preferred_element_type=F32)
    hit = rank == place.astype(F32)
    rest = weight_ref[...]
    acc = jnp.zeros(out_ref.shape, F32)
    for _ in range(3):
        piece = rest.astype(BF)
        rest = rest - piece.astype(F32)
        wide = jnp.dot(piece, spread, preferred_element_type=F32)
        chosen = jnp.where(hit, wide, 0.0).astype(BF)
        acc += jnp.dot(chosen, rows_ref[...], preferred_element_type=F32)
    out_ref[...] = acc.astype(BF)


def mix(rank, weight, rows, slots):
    tokens = rank.shape[0]
    width = rows.shape[1]

    def kernel(*refs):
        mix_kernel(slots, *refs)

    return pl.pallas_call(
        kernel,
        out_shape=jax.ShapeDtypeStruct((tokens, width), BF),
        compiler_params=pltpu.CompilerParams(vmem_limit_bytes=VMEM_LIMIT),
        cost_estimate=pl.CostEstimate(
            flops=6 * tokens * rows.shape[0] * width, bytes_accessed=1 << 20, transcendentals=0
        ),
        name="mix",
    )(rank, weight, rows)


def reorder_kernel(index_ref, in_ref, out_ref):
    for j in range(in_ref.shape[0]):
        out_ref[j] = in_ref[index_ref[j]]


def reorder(pieces, index):
    return pl.pallas_call(
        reorder_kernel,
        in_specs=[
            pl.BlockSpec(memory_space=pltpu.SMEM),
            pl.BlockSpec(memory_space=pltpu.VMEM),
        ],
        out_shape=jax.ShapeDtypeStruct(pieces.shape, pieces.dtype),
        compiler_params=pltpu.CompilerParams(vmem_limit_bytes=VMEM_LIMIT),
        cost_estimate=pl.CostEstimate(
            flops=0, bytes_accessed=2 * pieces.size * pieces.dtype.itemsize, transcendentals=0
        ),
        name="reorder",
    )(index, pieces)


def swap(pieces):
    return lax.all_to_all(pieces, "expert", split_axis=0, concat_axis=0, tiled=True)


def per_device(
    tokens,
    route_weight,
    route_expert,
    cotangent,
    gate_quant,
    up_quant,
    gate_scale,
    up_scale,
    down_quant,
    down_scale,
    first_moment,
    second_moment,
    old_expert,
    new_holder,
):
    number = lax.axis_size("expert")
    me = lax.axis_index("expert")
    tok_rows, top_count = route_expert.shape
    width = cotangent.shape[1]
    slots = min(tok_rows, tok_rows * top_count // number * 4 // 3)
    hidden_total = down_quant.shape[1]
    labels = jnp.arange(number, dtype=jnp.int32)
    giver = jnp.sum((new_holder[:, None] == labels[None, :]) * labels[:, None], axis=0)
    held = jnp.sum((new_holder[:, None] == labels[None, :]) * old_expert[:, None], axis=0)
    mine = labels == me
    expert_before = jnp.sum(jnp.where(mine, old_expert, 0))
    expert_after = jnp.sum(jnp.where(mine, held, 0))
    my_giver = jnp.sum(jnp.where(mine, giver, 0))

    scale_parts = jnp.concatenate(split_bits(down_scale[0]), axis=1)
    scale_rows, scale_cols = scale_parts.shape
    extra = jnp.concatenate(
        [
            route_expert.astype(BF),
            *split_bits(route_weight),
            jnp.pad(scale_parts, ((0, tok_rows - scale_rows), (0, QB - 4 * top_count - scale_cols))),
        ],
        axis=1,
    )
    gathered = lax.all_gather(jnp.concatenate([tokens, extra], axis=1), "expert", axis=0)
    table = gathered[:, :, width:].astype(F32)
    routes = table[:, :, :top_count]
    weights = (
        table[:, :, top_count : 2 * top_count]
        + table[:, :, 2 * top_count : 3 * top_count]
        + table[:, :, 3 * top_count : 4 * top_count]
    )
    third = scale_cols // 3
    scales = table[:, :scale_rows, 4 * top_count : 4 * top_count + scale_cols]
    scales = scales[:, :, :third] + scales[:, :, third : 2 * third] + scales[:, :, 2 * third :]
    new_scale = jnp.sum(jnp.where((labels == my_giver)[:, None, None], scales, 0.0), axis=0)
    rank_before = ranks(jnp.sum(jnp.where(routes == expert_before.astype(F32), 1.0, 0.0), axis=2))
    hit_after = routes == expert_after.astype(F32)
    rank_after = ranks(jnp.sum(jnp.where(hit_after, 1.0, 0.0), axis=2))
    weight_after = jnp.sum(jnp.where(hit_after, weights, 0.0), axis=2)

    piece_rows = hidden_total // number
    state = jnp.stack(
        [
            first_moment[0].astype(BF).reshape(number, piece_rows, width),
            second_moment[0].astype(BF).reshape(number, piece_rows, width),
            down_quant[0].reshape(number, piece_rows, width),
        ],
        axis=1,
    )
    spread = swap(state)

    cot_all = lax.all_gather(cotangent, "expert", axis=0)

    sent = compact(rank_before, gathered, slots, width)
    rows_in = lax.all_gather(sent, "dp", axis=0)
    hidden_part = gate_up(
        rows_in, gate_quant[0], up_quant[0], gate_scale.reshape(-1), up_scale.reshape(-1)
    )
    hidden_part, spread = lax.optimization_barrier((hidden_part, spread))
    state = swap(reorder(spread, giver))
    hidden_part = hidden_part.reshape(number, slots, -1)
    hidden_part = swap(reorder(swap(hidden_part), giver)).reshape(number * slots, -1)
    hidden = lax.all_gather(hidden_part, "dp", axis=0)

    out_rows = down(hidden, state, new_scale)
    returned = swap(out_rows.reshape(number, slots, width)).reshape(-1, width)
    back = weighted_compact(rank_after, weight_after, cot_all, slots, width)
    fresh, first_new, second_new = grad_adam(hidden, back, state, new_scale)

    chosen = route_expert[:, :, None] == held[None, None, :]
    own_rank = ranks(jnp.sum(chosen.astype(F32), axis=1).T).T
    own_weight = jnp.sum(jnp.where(chosen, route_weight[:, :, None], 0.0), axis=1)
    mixed = mix(own_rank, own_weight, returned, slots)
    return (mixed, fresh, first_new, second_new)


def solution(mesh):
    in_specs = (
        P("expert", "dp"),
        P("expert", None),
        P("expert", None),
        P("expert", "dp"),
        P("expert", None, "dp"),
        P("expert", None, "dp"),
        P("expert", None, "dp"),
        P("expert", None, "dp"),
        P("expert", None, "dp"),
        P("expert", None, "dp"),
        P("expert", None, "dp"),
        P("expert", None, "dp"),
        P(),
        P(),
    )
    out_specs = (
        P("expert", "dp"),
        P("expert", None, "dp"),
        P("expert", None, "dp"),
        P("expert", None, "dp"),
    )
    return jax.shard_map(
        per_device, mesh=mesh, in_specs=in_specs, out_specs=out_specs, check_vma=False
    )
```

time: 706 us -> 366 us (0.52); the launches traced: 697 us -> 365 us
  local copies, waits for them, and re-layouts: 160 us -> 11.3 us
  waiting for transfers between devices: 376 us -> 243 us
  starting transfers between devices: 72.3 us -> 19.5 us
  Pallas kernels: 0 us -> 31.2 us
  matrix products: 24 us -> 0.45 us
  other arithmetic: 34.7 us -> 13.1 us
  blocking collectives: 15.2 us -> 31.5 us
    all_to_all x7 -> x3, waiting for transfers between devices: 347 us -> 67 us  [swap(): lax.all_to_all(pieces, 'expert', split_axis=0, concat_axis=0, tiled=True)]
    all_gather x1 -> x4, waiting for transfers between devices: 28.9 us -> 175 us  [the longest x1 79 us: per_device(): lax.all_gather(jnp.concatenate([tokens, extra], axis=1), 'expert', axis=0)]
    unnamed x47 -> x31, local copies, waits for them, and re-layouts: 76.8 us -> 9.05 us
    all_to_all x7 -> x3, starting transfers between devices: 72.1 us -> 19.4 us  [swap(): lax.all_to_all(pieces, 'expert', split_axis=0, concat_axis=0, tiled=True)]
    all_to_all x0 -> x2, blocking collectives: none -> 31.5 us  [swap(): lax.all_to_all(pieces, 'expert', split_axis=0, concat_axis=0, tiled=True)]
    pallas_call x0 -> x8, Pallas kernels: none -> 31.2 us  [the longest x1 8.27 us: grad_adam(): pl.pallas_call(adam_kernel, grid=(parts,), in_specs=[pl.BlockSpec(memory_...]
    gather x6 -> x0, local copies, waits for them, and re-layouts: 30.9 us -> none  [the longest x1 7.82 us: per_device(): jnp.take(whole_tokens, token_ids, axis=0)]
    dot_general x4 -> x3, matrix products: 24 us -> 0.45 us  [ranks(): position = jnp.dot(mask.astype(BF), earlier, preferred_element_type=F32)]
  transfers between devices with their start and end apart: 8 -> 7, of which waited for: 7 -> 6; matrix products, arithmetic and copies ran while one was open for 27% -> 2% of each run, Pallas kernels for 0% -> 8%
where the time goes in v1:
time: 366 us; the launch traced here: 365 us
  waiting for transfers between devices  243 us (66%)
  blocking collectives  31.5 us (9%)
  Pallas kernels  31.2 us (9%)
  starting transfers between devices  19.5 us (5%)
  between operations  15.2 us (4%)
  other arithmetic  13.1 us (4%)
  local copies, waits for them, and re-layouts  11.3 us (3%)
    all_gather x1, waiting for transfers between devices, per_device(): lax.all_gather(jnp.concatenate([tokens, extra], axis=1), 'expert', axis=0)  79 us
    all_to_all x3, waiting for transfers between devices, swap(): lax.all_to_all(pieces, 'expert', split_axis=0, concat_axis=0, tiled=True)  67 us
    all_gather x1, waiting for transfers between devices, per_device(): rows_in = lax.all_gather(sent, 'dp', axis=0)  41.8 us
    all_gather x1, waiting for transfers between devices, per_device(): cot_all = lax.all_gather(cotangent, 'expert', axis=0)  36.4 us
    all_to_all x2, blocking collectives, swap(): lax.all_to_all(pieces, 'expert', split_axis=0, concat_axis=0, tiled=True)  31.5 us
    all_to_all x3, starting transfers between devices, swap(): lax.all_to_all(pieces, 'expert', split_axis=0, concat_axis=0, tiled=True)  19.4 us
    all_gather x1, waiting for transfers between devices, per_device(): hidden = lax.all_gather(hidden_part, 'dp', axis=0)  17.9 us
    unnamed x31, local copies, waits for them, and re-layouts  9.05 us
  transfers between devices with their start and end apart: 7, of which 6 were waited for; matrix products, arithmetic and copies ran while one was open for 2% of the time, Pallas kernels for 8%

profile of v1, /device:TPU:1, one launch (start us, length us, event | category | flops | bytes accessed | tf_op | source)
XLA Modules:
  0.0 365.0 jit_solution(17435482017189170104)
XLA Ops:
  8.0 0.7 fusion.11
  9.1 0.7 reduce-precision_convert_fusion.3
  9.9 1.6 concatenate.7
  11.6 0.8 select_reduce_fusion.2
  12.3 1.3 select_reduce_fusion.4
  14.9 79.0 %all-gather.10.cloned.1.call-done = bf16[3072,640]{1,0:T(8,128)(2,1)} async-done(((bf16[96,640]{1,0:T(8,128)(2,1)}), bf16[3072,640]{1,0:T(8,128)(2,1)}) %all-gather.10.cloned.1.call-update) | async-done | bytes 3932176 | tf_op jit(solution)/shard_map/all_gather | solution.py:347
  93.9 1.3 slice_convert_fusion
  95.3 2.7 fusion.1
  98.1 1.5 compact.1
  100.0 1.5 copy-done.11
  101.5 1.1 copy-done.12
  102.6 2.0 pad_maximum_fusion
  104.7 5.8 %all-to-all-start = ((bf16[32,3,32,512]{3,2,1,0:T(8,128)(2,1)}), bf16[32,3,32,512]{3,2,1,0:T(8,128)(2,1)}, u32[]{:S(2)}, u32[]{:S(2)}) async-start(bf16[32,3,32,512]{3,2,1,0:T(8,128)(2,1)} %pad_maximum_fusion), calls=%async_computation | async-start | bytes 6291456 | tf_op jit(solution)/shard_map/all_to_all | solution.py:304
  110.5 41.8 %all-gather.12.cloned.1.call-done = bf16[8192,512]{1,0:T(8,128)(2,1)} async-done(((bf16[1024,512]{1,0:T(8,128)(2,1)}), bf16[8192,512]{1,0:T(8,128)(2,1)}) %all-gather.12.cloned.1.call-update) | async-done | bytes 8388624 | tf_op jit(solution)/shard_map/all_gather | solution.py:378
  152.3 7.7 %gate_up.1 = bf16[1024,128]{1,0:T(8,128)(2,1)S(1)} custom-call(f32[32]{0:T(128)S(1)} %bitcast.28, f32[32]{0:T(128)S(1)} %bitcast.29, bf16[8,1024,512]{2,1,0:T(8,128)(2,1)} %bitcast.30, bf16[4096,128]{1,0:T(8,128)(2,1)S(1)} %bitcast.26, bf16[4096,128]{1,0:T(8,128)(2,1)S(1)} %bitcast.27), custom_call_target="tpu_custom_call" | custom-call | flops 2147483648 | bytes 11534336 | tf_op jit(solution)/shard_map/gate_up/pallas_call | solution.py:129
  160.1 19.1 %all-to-all-done.in_ref = bf16[32,3,32,512]{3,2,1,0:T(8,128)(2,1)} async-done(((bf16[32,3,32,512]{3,2,1,0:T(8,128)(2,1)}), bf16[32,3,32,512]{3,2,1,0:T(8,128)(2,1)}, u32[]{:S(2)}, u32[]{:S(2)}) %all-to-all-start) | async-done | bytes 3145760 | tf_op jit(solution)/shard_map/all_to_all | solution.py:304
  179.1 17.4 %all_to_all.25.in_ref = bf16[32,32,128]{2,1,0:T(8,128)(2,1)S(1)} all-to-all(bf16[32,32,128]{2,1,0:T(8,128)(2,1)S(1)} %bitcast.25), channel_id=1, replica_groups=mesh['expert'=32,'dp'=8] {'expert'}, dimensions={0} | all-to-all | bytes 524288 | tf_op jit(solution)/shard_map/all_to_all | solution.py:304
  197.1 14.1 %all_to_all.26 = bf16[32,32,128]{2,1,0:T(8,128)(2,1)} all-to-all(bf16[32,32,128]{2,1,0:T(8,128)(2,1)S(1)} %reorder.2), channel_id=1, replica_groups=mesh['expert'=32,'dp'=8] {'expert'}, dimensions={0} | all-to-all | bytes 524288 | tf_op jit(solution)/shard_map/all_to_all | solution.py:304
  211.2 3.8 %reorder.3 = bf16[32,3,32,512]{3,2,1,0:T(8,128)(2,1)} custom-call(s32[32]{0:T(128)S(1)} %get-tuple-element.19.index_ref, bf16[32,3,32,512]{3,2,1,0:T(8,128)(2,1)} %all-to-all-done.in_ref), custom_call_target="tpu_custom_call" | custom-call | bytes 6291456 | tf_op jit(solution)/shard_map/reorder/pallas_call | solution.py:288
  215.0 4.1 %all-to-all-start.3 = ((bf16[32,3,32,512]{3,2,1,0:T(8,128)(2,1)}), bf16[32,3,32,512]{3,2,1,0:T(8,128)(2,1)S(1)}, u32[]{:S(2)}, u32[]{:S(2)}) async-start(bf16[32,3,32,512]{3,2,1,0:T(8,128)(2,1)} %reorder.3), calls=%async_computation.3 | async-start | bytes 6291456 | tf_op jit(solution)/shard_map/all_to_all | solution.py:304
  221.0 1.3 fusion.5.scale_ref
  222.2 17.9 %all-gather.8.cloned.1.call-done.hidden_ref = bf16[8,1024,128]{2,1,0:T(8,128)(2,1)} async-done(((bf16[1,1024,128]{2,1,0:T(8,128)(2,1)}), bf16[8,1024,128]{2,1,0:T(8,128)(2,1)}) %all-gather.8.cloned.1.call-update) | async-done | bytes 2097168 | tf_op jit(solution)/shard_map/all_gather | solution.py:386
  240.2 47.9 %all-to-all-done.3.quant_ref.state_ref = bf16[32,3,32,512]{3,2,1,0:T(8,128)(2,1)S(1)} async-done(((bf16[32,3,32,512]{3,2,1,0:T(8,128)(2,1)}), bf16[32,3,32,512]{3,2,1,0:T(8,128)(2,1)S(1)}, u32[]{:S(2)}, u32[]{:S(2)}) %all-to-all-start.3) | async-done | bytes 3145760 | tf_op jit(solution)/shard_map/all_to_all | solution.py:304
  288.1 1.7 copy-done.9
  289.8 1.6 copy-done
  291.4 7.2 %down.1 = bf16[1024,512]{1,0:T(8,128)(2,1)} custom-call(f32[8,4]{1,0:T(8,128)S(1)} %fusion.5.scale_ref, bf16[8,1024,128]{2,1,0:T(8,128)(2,1)S(1)} %copy-done, bf16[32,3,32,512]{3,2,1,0:T(8,128)(2,1)} %copy-done.9), custom_call_target="tpu_custom_call" | custom-call | flops 1073741824 | bytes 4194304 | tf_op jit(solution)/shard_map/down/pallas_call | solution.py:178
  298.6 9.5 %all-to-all-start.4 = ((bf16[32,32,512]{2,1,0:T(8,128)(2,1)}), bf16[32,32,512]{2,1,0:T(8,128)(2,1)S(1)}, u32[]{:S(2)}, u32[]{:S(2)}) async-start(bf16[32,32,512]{2,1,0:T(8,128)(2,1)} %bitcast.12), calls=%async_computation.4 | async-start | bytes 2097152 | tf_op jit(solution)/shard_map/all_to_all | solution.py:304
  308.7 36.4 %all-gather.14.cloned.1.call-done = bf16[3072,512]{1,0:T(8,128)(2,1)} async-done(((bf16[96,512]{1,0:T(8,128)(2,1)}), bf16[3072,512]{1,0:T(8,128)(2,1)}) %all-gather.14.cloned.1.call-update) | async-done | bytes 3145744 | tf_op jit(solution)/shard_map/all_gather | solution.py:375
  345.1 1.9 copy-done.3
  347.6 1.0 copy-done.1
  348.6 8.3 %grad_adam.1 = (bf16[1,1024,512]{2,1,0:T(8,128)(2,1)}, f32[1,1024,512]{2,1,0:T(8,128)}, f32[1,1024,512]{2,1,0:T(8,128)}) custom-call(f32[8,4]{1,0:T(8,128)S(1)} %fusion.5.scale_ref, bf16[8,1024,128]{2,1,0:T(8,128)(2,1)S(1)} %copy-done.1, bf16[1024,512]{1,0:T(8,128)(2,1)S(1)} %back_rows.1.back_ref, bf16[32,3,32,512]{3,2,1,0:T(8,128)(2,1)} %copy-done.9), custom_call_target="tpu_custom_call" | custom-call | flops 1073741824 | bytes 11534336 | tf_op jit(solution)/shard_map/grad_adam/pallas_call | solution.py:221
  356.9 1.6 mix.1
  (53 shorter events, 5.6 us)
Async XLA Ops:
  7.2 86.8 %all-gather.10.cloned.1.call-start = ((), (), s32[]{:S(2)}) async-start(), calls=%async_computation.6 | async-start | bytes 4055040 | tf_op jit(solution)/shard_map/all_gather | solution.py:347
  11.5 140.8 %all-gather.12.cloned.1.call-start = ((), (), s32[]{:S(2)}) async-start(), calls=%async_computation.7 | async-start | bytes 9437184 | tf_op jit(solution)/shard_map/all_gather | solution.py:378
  95.2 2.7 copy-start.8
  95.2 2.8 copy-start.2
  98.1 1.7 copy-start.10
  99.8 1.6 copy-start.11
  101.4 1.2 copy-start.12
  104.7 47.6 %copy-start.4 = (bf16[1,4096,128]{2,1,0:T(8,128)(2,1)S(1)}, bf16[1,4096,128]{2,1,0:T(8,128)(2,1)}, u32[]{:S(2)}) copy-start(bf16[1,4096,128]{2,1,0:T(8,128)(2,1)} %param.18) | copy-start | bytes 3145732
  104.7 47.7 %copy-start.5 = (bf16[1,4096,128]{2,1,0:T(8,128)(2,1)S(1)}, bf16[1,4096,128]{2,1,0:T(8,128)(2,1)}, u32[]{:S(2)}) copy-start(bf16[1,4096,128]{2,1,0:T(8,128)(2,1)} %param.19) | copy-start | bytes 3145732
  104.7 47.7 %copy-start.6 = (f32[1,32,1]{1,2,0:T(1,128)S(1)}, f32[1,32,1]{1,2,0:T(1,128)}, u32[]{:S(2)}) copy-start(f32[1,32,1]{1,2,0:T(1,128)} %param.20) | copy-start | bytes 388
  104.7 47.7 %copy-start.7 = (f32[1,32,1]{1,2,0:T(1,128)S(1)}, f32[1,32,1]{1,2,0:T(1,128)}, u32[]{:S(2)}) copy-start(f32[1,32,1]{1,2,0:T(1,128)} %param.21) | copy-start | bytes 388
  104.7 74.4 %all-to-all-start = ((bf16[32,3,32,512]{3,2,1,0:T(8,128)(2,1)}), bf16[32,3,32,512]{3,2,1,0:T(8,128)(2,1)}, u32[]{:S(2)}, u32[]{:S(2)}) async-start(bf16[32,3,32,512]{3,2,1,0:T(8,128)(2,1)} %pad_maximum_fusion), calls=%async_computation | async-start | bytes 6291456 | tf_op jit(solution)/shard_map/all_to_all | solution.py:304
  110.5 129.7 %all-gather.8.cloned.1.call-start = ((), (), s32[]{:S(2)}) async-start(), calls=%async_computation.5 | async-start | bytes 2359296 | tf_op jit(solution)/shard_map/all_gather | solution.py:386
  215.0 73.1 %all-to-all-start.3 = ((bf16[32,3,32,512]{3,2,1,0:T(8,128)(2,1)}), bf16[32,3,32,512]{3,2,1,0:T(8,128)(2,1)S(1)}, u32[]{:S(2)}, u32[]{:S(2)}) async-start(bf16[32,3,32,512]{3,2,1,0:T(8,128)(2,1)} %reorder.3), calls=%async_computation.3 | async-start | bytes 6291456 | tf_op jit(solution)/shard_map/all_to_all | solution.py:304
  219.1 126.0 %all-gather.14.cloned.1.call-start = ((), (), s32[]{:S(2)}) async-start(), calls=%async_computation.8 | async-start | bytes 3244032 | tf_op jit(solution)/shard_map/all_gather | solution.py:375
  288.1 1.7 copy-start.9
  289.8 1.6 copy-start
  298.6 9.5 %copy-start.13 = (f32[96,8]{0,1:T(8,128)S(1)}, f32[96,8]{0,1:T(8,128)}, u32[]{:S(2)}) copy-start(f32[96,8]{0,1:T(8,128)} %param.15) | copy-start | bytes 9220
  298.6 9.5 %copy-start.14 = (s32[96,8]{0,1:T(8,128)S(1)}, s32[96,8]{0,1:T(8,128)}, u32[]{:S(2)}) copy-start(s32[96,8]{0,1:T(8,128)} %param.16) | copy-start | bytes 9220
  298.6 58.3 %all-to-all-start.4 = ((bf16[32,32,512]{2,1,0:T(8,128)(2,1)}), bf16[32,32,512]{2,1,0:T(8,128)(2,1)S(1)}, u32[]{:S(2)}, u32[]{:S(2)}) async-start(bf16[32,32,512]{2,1,0:T(8,128)(2,1)} %bitcast.12), calls=%async_computation.4 | async-start | bytes 2097152 | tf_op jit(solution)/shard_map/all_to_all | solution.py:304
  345.1 1.9 copy-start.3
  347.0 1.6 copy-start.1
Sparse Core Ops, SparseCore 0:
  11.7 82.2 all-gather.9
  99.7 52.5 all-gather.11
  211.4 28.7 all-gather.7
  242.6 102.4 all-gather.13

commit v2 on v0

v2 whole, which is shorter than its diff:
```python
import jax
import jax.numpy as jnp
from jax import lax
from jax.experimental import pallas as pl
from jax.experimental.pallas import tpu as pltpu
from jax.sharding import PartitionSpec as P

QB = 128
BF = jnp.bfloat16
F32 = jnp.float32
MESH = pl.DeviceIdType.MESH

beta_first = 0.9
beta_second = 0.95
adam_eps = 1e-08
learn_rate = 0.003
decay_rate = 0.1
step_count = 20
fix_first = 1.0 - beta_first**step_count
fix_second = 1.0 - beta_second**step_count

VMEM_LIMIT = 58 * 1024 * 1024

T, SC, D1, F1, S1, B, D2, F2, S2, H1, H2, O, Y1, Y2, W = range(15)
KINDS = 15


def transposed_dot(a, b):
    return lax.dot_general(a, b, (((0,), (0,)), ((), ())), preferred_element_type=F32)


def step_kernel(
    giver_ref,
    my_giver_ref,
    gate_scale_ref,
    up_scale_ref,
    before_ref,
    after_ref,
    route_ref,
    weight_ref,
    tok_ref,
    cot_ref,
    scale_ref,
    gate_hbm,
    up_hbm,
    down_hbm,
    first_hbm,
    second_hbm,
    mixed_ref,
    fresh_ref,
    first_ref,
    second_ref,
    tok_send,
    tok_recv,
    scale_all,
    down_mid,
    first_send,
    first_mid,
    second_send,
    second_mid,
    back_send,
    back_recv,
    down_out,
    down_new,
    first_out,
    first_new,
    second_out,
    second_new,
    hid_send,
    hid_mid,
    hid_out,
    hid_new,
    out_send,
    out_recv,
    rows_all,
    weights_all,
    gate_v,
    up_v,
    hidden_all,
    grad_ref,
    pick_ref,
    send_sem,
    recv_sem,
    local_sem,
    load_sem,
):
    number = lax.axis_size("expert")
    parts = lax.axis_size("dp")
    cores = weights_all.shape[0]
    e = lax.axis_index("expert")
    d = lax.axis_index("dp")
    core = lax.rem(d, cores)
    tokens, width = tok_ref.shape
    slots = tok_send.shape[1]
    total = number * slots
    half = number // cores
    half_rows = half * slots
    hidden_part = gate_v.shape[1]

    def remote(src, dst, kind, target):
        return pltpu.make_async_remote_copy(
            src_ref=src,
            dst_ref=dst,
            send_sem=send_sem.at[kind],
            recv_sem=recv_sem.at[kind],
            device_id=target,
            device_id_type=MESH,
        )

    loads = [
        pltpu.make_async_copy(src, dst, load_sem.at[i])
        for i, (src, dst) in enumerate(
            [
                (gate_hbm, gate_v),
                (up_hbm, up_v),
                (first_hbm, first_ref),
                (second_hbm, second_ref),
            ]
        )
    ]
    for load in loads:
        load.start()

    barrier = pltpu.get_barrier_semaphore()

    def greet_expert(k, carry):
        pl.semaphore_signal(
            barrier, inc=1, device_id=(lax.rem(e + k, number), d), device_id_type=MESH
        )
        return carry

    def greet_dp(k, carry):
        pl.semaphore_signal(
            barrier, inc=1, device_id=(e, lax.rem(d + k, parts)), device_id_type=MESH
        )
        return carry

    lax.fori_loop(1, number, greet_expert, 0)
    lax.fori_loop(1, parts, greet_dp, 0)

    i = lax.broadcasted_iota(jnp.int32, (tokens, tokens), 0)
    j = lax.broadcasted_iota(jnp.int32, (tokens, tokens), 1)
    earlier = (j < i).astype(BF)
    holder = lax.broadcasted_iota(jnp.int32, (number, total), 0)
    column = lax.broadcasted_iota(jnp.int32, (number, total), 1)
    spread = jnp.logical_and(column >= holder * slots, column < (holder + 1) * slots).astype(BF)
    place = lax.rem(lax.broadcasted_iota(jnp.int32, (tokens, total), 1), slots).astype(F32)

    def slot_hits(hit):
        rank = jnp.dot(earlier, hit.astype(BF), preferred_element_type=F32)
        rank = jnp.where(hit > 0.0, rank, -1.0)
        return jnp.dot(rank.astype(BF), spread, preferred_element_type=F32) == place

    routes = route_ref[...]
    hit_before = jnp.zeros((tokens, number), F32)
    hit_after = jnp.zeros((tokens, number), F32)
    weight_after = jnp.zeros((tokens, number), F32)
    for k in range(routes.shape[1]):
        named = routes[:, k : k + 1]
        hit_before += (named == before_ref[...]).astype(F32)
        match = named == after_ref[...]
        hit_after += match.astype(F32)
        weight_after += jnp.where(match, weight_ref[:, k : k + 1], 0.0)

    pick = slot_hits(hit_before).astype(BF)
    tok_send[...] = transposed_dot(pick, tok_ref[...]).astype(BF).reshape(tok_send.shape)

    pl.semaphore_wait(barrier, number - 1 + parts - 1)

    def send_all(src, dst, kind, same=False):
        def body(k, carry):
            t = lax.rem(e + k, number)
            remote(src if same else src.at[t], dst.at[e], kind, (t, d)).start()
            return carry

        lax.fori_loop(1, number, body, 0)
        pltpu.make_async_copy(src if same else src.at[e], dst.at[e], local_sem.at[kind]).start()

    def wait_all(src, dst, kind, same=False):
        rest = dst.at[pl.ds(0, number - 1)]
        remote(rest, rest, kind, (lax.rem(e + 1, number), d)).wait_recv()
        pltpu.make_async_copy(src if same else src.at[e], dst.at[e], local_sem.at[kind]).wait()

    def sent_all(dst, kind):
        rest = dst.at[pl.ds(0, number - 1)]
        remote(rest, rest, kind, (lax.rem(e + 1, number), d)).wait_send()

    def reorder(src, dst):
        def body(k, carry):
            dst[k] = src[giver_ref[k]]
            return carry

        lax.fori_loop(0, number, body, 0)

    send_all(tok_send, tok_recv, T)
    send_all(scale_ref, scale_all, SC, same=True)

    loads[0].wait()
    loads[1].wait()

    def dequantize(r, carry):
        rows = pl.ds(pl.multiple_of(r * QB, QB), QB)
        gate = (gate_v[rows, :].astype(F32) * gate_scale_ref[r]).astype(BF)
        up = (up_v[rows, :].astype(F32) * up_scale_ref[r]).astype(BF)
        weights_all[core, rows, :] = jnp.concatenate([gate, up], axis=1)
        return carry

    lax.fori_loop(0, gate_v.shape[0] // QB, dequantize, 0)
    sibling = (e, d + 1 - 2 * core)
    weights_copy = remote(weights_all.at[core], weights_all.at[core], W, sibling)
    weights_copy.start()

    hit_slots = slot_hits(hit_after)
    rest = weight_after
    for p in range(3):
        piece = rest.astype(BF)
        rest = rest - piece.astype(F32)
        wide = jnp.dot(piece, spread, preferred_element_type=F32)
        pick_ref[p] = jnp.where(hit_slots, wide, 0.0).astype(BF)

    loads[2].wait()
    first_send[...] = first_ref[...].astype(BF).reshape(first_send.shape)
    loads[3].wait()
    second_send[...] = second_ref[...].astype(BF).reshape(second_send.shape)

    sent_all(tok_recv, T)
    send_all(down_hbm, down_mid, D1)
    back = transposed_dot(pick_ref[0], cot_ref[...])
    back += transposed_dot(pick_ref[1], cot_ref[...])
    back += transposed_dot(pick_ref[2], cot_ref[...])
    back_send[...] = back.astype(BF).reshape(back_send.shape)

    wait_all(tok_send, tok_recv, T)

    def send_rows(k, carry):
        t = lax.rem(d + k, parts)
        src = tok_recv.at[pl.ds(lax.rem(t, cores) * half, half)]
        remote(src, rows_all.at[d], Y1, (e, t)).start()
        return carry

    lax.fori_loop(1, parts, send_rows, 0)
    own_rows = pltpu.make_async_copy(
        tok_recv.at[pl.ds(core * half, half)], rows_all.at[d], local_sem.at[Y1]
    )
    own_rows.start()
    send_all(first_send, first_mid, F1)
    send_all(second_send, second_mid, S1)
    send_all(back_send, back_recv, B)

    wait_all(down_hbm, down_mid, D1)
    reorder(down_mid, down_out)
    send_all(down_out, down_new, D2)

    own_rows.wait()
    weights_copy.wait()
    others = rows_all.at[pl.ds(0, parts - 1)]
    remote(others, others, Y1, sibling).wait()
    for c in range(cores):
        value = jnp.zeros((half_rows, 2 * hidden_part), F32)
        for k in range(parts):
            value += jnp.dot(
                rows_all[k].reshape(half_rows, width),
                weights_all[c, k * width : (k + 1) * width, :],
                preferred_element_type=F32,
            )
        gate = value[:, :hidden_part]
        up = value[:, hidden_part:]
        act = (gate / (1.0 + jnp.exp(-gate)) * up).astype(BF)
        hid_send[:, :, c * hidden_part : (c + 1) * hidden_part] = act.reshape(
            number, half_rows // number, hidden_part
        )
    send_all(hid_send, hid_mid, H1)

    wait_all(first_send, first_mid, F1)
    reorder(first_mid, first_out)
    send_all(first_out, first_new, F2)

    wait_all(hid_send, hid_mid, H1)
    reorder(hid_mid, hid_out)
    send_all(hid_out, hid_new, H2)

    wait_all(second_send, second_mid, S1)
    reorder(second_mid, second_out)
    send_all(second_out, second_new, S2)

    wait_all(hid_out, hid_new, H2)

    def send_hidden(k, carry):
        remote(hid_new, hidden_all.at[d], Y2, (e, lax.rem(d + k, parts))).start()
        return carry

    lax.fori_loop(1, parts, send_hidden, 0)
    own_hidden = pltpu.make_async_copy(hid_new, hidden_all.at[d], local_sem.at[Y2])
    own_hidden.start()

    wait_all(scale_ref, scale_all, SC, same=True)
    wait_all(down_out, down_new, D2)
    scale = scale_all[my_giver_ref[0]]
    scale_wide = jnp.concatenate(
        [jnp.broadcast_to(scale[:, c : c + 1], (scale.shape[0], QB)) for c in range(width // QB)],
        axis=1,
    )
    pieces = QB // down_new.shape[1]

    def master_rows(r):
        quant = down_new[r * pieces : (r + 1) * pieces].reshape(QB, width)
        return quant.astype(F32) * scale_wide[r : r + 1, :]

    own_hidden.wait()
    others = hidden_all.at[pl.ds(0, parts - 1)]
    remote(others, others, Y2, sibling).wait()
    pair = cores * hidden_part
    for c in range(cores):
        value = jnp.zeros((half_rows, width), F32)
        for y in range(parts // cores):
            down_w = jnp.concatenate(
                [master_rows(y * pair // QB + r).astype(BF) for r in range(pair // QB)], axis=0
            )
            value += jnp.dot(
                hidden_all[y * cores + c].reshape(half_rows, pair),
                down_w,
                preferred_element_type=F32,
            )
        out_send[c * half : (c + 1) * half] = value.astype(BF).reshape(half, slots, width)
    send_all(out_send, out_recv, O)

    wait_all(back_send, back_recv, B)
    for y in range(parts // cores):
        value = jnp.zeros((pair, width), F32)
        for c in range(cores):
            value += transposed_dot(
                hidden_all[y * cores + c].reshape(half_rows, pair),
                back_recv[c * half : (c + 1) * half].reshape(half_rows, width),
            )
        grad_ref[y * pair : (y + 1) * pair, :] = value

    wait_all(first_out, first_new, F2)
    wait_all(second_out, second_new, S2)
    for r in range(grad_ref.shape[0] // QB):
        rows = slice(r * QB, (r + 1) * QB)
        block = slice(r * pieces, (r + 1) * pieces)
        grad = grad_ref[rows, :]
        master = master_rows(r)
        first = first_new[block].reshape(QB, width).astype(F32)
        second = second_new[block].reshape(QB, width).astype(F32)
        first = beta_first * first + (1.0 - beta_first) * grad
        second = beta_second * second + (1.0 - beta_second) * grad * grad
        update = first / fix_first / (jnp.sqrt(second / fix_second) + adam_eps)
        fresh_ref[rows, :] = (master - learn_rate * (update + decay_rate * master)).astype(BF)
        first_ref[rows, :] = first
        second_ref[rows, :] = second

    wait_all(out_send, out_recv, O)
    returned = out_recv[...].reshape(total, width)
    value = jnp.dot(pick_ref[0], returned, preferred_element_type=F32)
    value += jnp.dot(pick_ref[1], returned, preferred_element_type=F32)
    value += jnp.dot(pick_ref[2], returned, preferred_element_type=F32)
    mixed_ref[...] = value.astype(BF)

    for dst, kind in (
        (scale_all, SC),
        (down_mid, D1),
        (first_mid, F1),
        (second_mid, S1),
        (back_recv, B),
        (down_new, D2),
        (first_new, F2),
        (second_new, S2),
        (hid_mid, H1),
        (hid_new, H2),
        (out_recv, O),
    ):
        sent_all(dst, kind)


def per_device(
    tokens,
    route_weight,
    route_expert,
    cotangent,
    gate_quant,
    up_quant,
    gate_scale,
    up_scale,
    down_quant,
    down_scale,
    first_moment,
    second_moment,
    old_expert,
    new_holder,
):
    number = lax.axis_size("expert")
    parts = lax.axis_size("dp")
    cores = 2
    me = lax.axis_index("expert")
    tok_rows, top_count = route_expert.shape
    width = cotangent.shape[1]
    slots = min(tok_rows, tok_rows * top_count // number * 4 // 3)
    model_width, hidden_part = gate_quant.shape[1:]
    hidden_total = down_quant.shape[1]
    piece_rows = hidden_total // number
    labels = jnp.arange(number, dtype=jnp.int32)
    takes = new_holder[:, None] == labels[None, :]
    giver = jnp.sum(takes * labels[:, None], axis=0)
    held = jnp.sum(takes * old_expert[:, None], axis=0)
    my_giver = jnp.sum(jnp.where(new_holder == me, labels, 0)).reshape(1)
    scale = jnp.pad(down_scale[0], ((0, 0), (0, QB - down_scale.shape[2])))

    smem = pl.BlockSpec(memory_space=pltpu.SMEM)
    vmem = pl.BlockSpec(memory_space=pltpu.VMEM)
    hbm = pl.BlockSpec(memory_space=pl.ANY)
    state = pltpu.VMEM((number, piece_rows, width), BF)
    rows = pltpu.VMEM((number, slots, width), BF)
    half_rows = number * slots // cores
    hid = pltpu.VMEM((number, half_rows // number, cores * hidden_part), BF)
    mixed, fresh, first_new, second_new = pl.pallas_call(
        step_kernel,
        in_specs=[smem] * 4 + [vmem] * 7 + [hbm] * 5,
        out_specs=[vmem] * 4,
        out_shape=[
            jax.ShapeDtypeStruct((tok_rows, width), BF),
            jax.ShapeDtypeStruct((hidden_total, width), BF),
            jax.ShapeDtypeStruct((hidden_total, width), F32),
            jax.ShapeDtypeStruct((hidden_total, width), F32),
        ],
        scratch_shapes=[
            rows,
            rows,
            pltpu.VMEM((number,) + scale.shape, F32),
            state,
            state,
            state,
            state,
            state,
            rows,
            rows,
            state,
            state,
            state,
            state,
            state,
            state,
            hid,
            hid,
            hid,
            hid,
            rows,
            rows,
            pltpu.VMEM((parts, number // cores, slots, width), BF),
            pltpu.VMEM((cores, model_width, 2 * hidden_part), BF),
            pltpu.VMEM((model_width, hidden_part), BF),
            pltpu.VMEM((model_width, hidden_part), BF),
            pltpu.VMEM((parts, number, half_rows // number, cores * hidden_part), BF),
            pltpu.VMEM((hidden_total, width), F32),
            pltpu.VMEM((3, tok_rows, number * slots), BF),
            pltpu.SemaphoreType.DMA((KINDS,)),
            pltpu.SemaphoreType.DMA((KINDS,)),
            pltpu.SemaphoreType.DMA((KINDS,)),
            pltpu.SemaphoreType.DMA((4,)),
        ],
        compiler_params=pltpu.CompilerParams(
            collective_id=0, has_side_effects=True, vmem_limit_bytes=VMEM_LIMIT
        ),
        name="step",
    )(
        giver,
        my_giver,
        gate_scale.reshape(-1),
        up_scale.reshape(-1),
        old_expert.reshape(1, number),
        held.reshape(1, number),
        route_expert,
        route_weight,
        tokens,
        cotangent,
        scale,
        gate_quant[0],
        up_quant[0],
        down_quant.reshape(number, piece_rows, width),
        first_moment[0],
        second_moment[0],
    )
    return (mixed, fresh[None], first_new[None], second_new[None])


def solution(mesh):
    in_specs = (
        P("expert", "dp"),
        P("expert", None),
        P("expert", None),
        P("expert", "dp"),
        P("expert", None, "dp"),
        P("expert", None, "dp"),
        P("expert", None, "dp"),
        P("expert", None, "dp"),
        P("expert", None, "dp"),
        P("expert", None, "dp"),
        P("expert", None, "dp"),
        P("expert", None, "dp"),
        P(),
        P(),
    )
    out_specs = (
        P("expert", "dp"),
        P("expert", None, "dp"),
        P("expert", None, "dp"),
        P("expert", None, "dp"),
    )
    return jax.shard_map(
        per_device, mesh=mesh, in_specs=in_specs, out_specs=out_specs, check_vma=False
    )
```

time: 706 us -> 255 us (0.36); the launches traced: 697 us -> 255 us
  waiting for transfers between devices: 376 us -> 0 us
  Pallas kernels: 0 us -> 239 us
  local copies, waits for them, and re-layouts: 160 us -> 11.8 us
  starting transfers between devices: 72.3 us -> 0 us
  other arithmetic: 34.7 us -> 2.65 us
  matrix products: 24 us -> 0 us
  blocking collectives: 15.2 us -> 0 us
  between operations: 14.6 us -> 0.66 us
    all_to_all x7 -> x0, waiting for transfers between devices: 347 us -> none  [the longest x1 143 us: per_device(): lax.all_to_all(sent_rows, 'expert', split_axis=0, concat_axis=0, tiled=True)]
    pallas_call x0 -> x1, Pallas kernels: none -> 239 us  [per_device(): pl.pallas_call(step_kernel, in_specs=[smem] * 4 + [vmem] * 7 + [hbm] * 5,...]
    all_to_all x7 -> x0, starting transfers between devices: 72.1 us -> none  [the longest x1 15.6 us: per_device(): lax.all_to_all(back_send, 'expert', split_axis=0, concat_axis=0, tiled=True)]
    unnamed x47 -> x10, local copies, waits for them, and re-layouts: 76.8 us -> 10.4 us
    gather x6 -> x0, local copies, waits for them, and re-layouts: 30.9 us -> none  [the longest x1 7.82 us: per_device(): jnp.take(whole_tokens, token_ids, axis=0)]
    all_gather x1 -> x0, waiting for transfers between devices: 28.9 us -> none  [per_device(): hidden_full = lax.all_gather(hidden_part, 'dp', axis=1, tiled=True)]
    dot_general x4 -> x0, matrix products: 24 us -> none  [the longest x1 9.34 us: per_device(): lax.dot_general(hidden_full, back_in, (((0,), (0,)), ((), ())), preferred...]
    select_n x7 -> x0, other arithmetic: 16 us -> none  [the longest x1 7.42 us: per_device(): jnp.take(whole_tokens, token_ids, axis=0)]
  transfers between devices with their start and end apart: 8 -> 0, of which waited for: 7 -> 0; matrix products, arithmetic and copies ran while one was open for 27% -> 0% of each run, Pallas kernels for 0% -> 0%
where the time goes in v2:
time: 255 us
  Pallas kernels  239 us (94%)
  local copies, waits for them, and re-layouts  11.8 us (5%)
  other arithmetic  2.65 us (1%)
    pallas_call x1, Pallas kernels, per_device(): pl.pallas_call(step_kernel, in_specs=[smem] * 4 + [vmem] * 7 + [hbm] * 5,...  239 us
    unnamed x10, local copies, waits for them, and re-layouts  10.4 us

profile of v2, /device:TPU:1, one launch (start us, length us, event | category | flops | bytes accessed | tf_op | source)
XLA Modules:
  0.0 254.5 jit_solution(7423464176205679203)
XLA Ops:
  0.6 1.4 fusion
  2.0 1.3 select_reduce_fusion
  3.3 0.8 copy.21
  4.0 0.6 pad.4.scale_ref
  4.6 1.4 copy.23.weight_ref
  6.0 1.4 copy.22.route_ref
  7.4 239.4 %step.1 = (bf16[96,512]{1,0:T(8,128)(2,1)}, bf16[1024,512]{1,0:T(8,128)(2,1)}, f32[1024,512]{1,0:T(8,128)}, f32[1024,512]{1,0:T(8,128)}) custom-call(s32[32]{0:T(128)} %get-tuple-element.13.giver_ref, s32[1]{0:T(128)} %bitcast.my_giver_ref, f32[32]{0:T(128)} %bitcast.25, f32[32]{0:T(128)} %bitcast.26, s32[1,32]{1,0:T(1,128)} %bitcast.22, s32[1,32]{1,0:T(1,128)} %bitcast.23, ...), custom_call_target="tpu_custom_call" | custom-call | tf_op jit(solution)/shard_map/step/pallas_call | solution.py:416
  246.9 0.0 copy-start.1
  246.9 1.7 copy.28
  248.6 2.3 copy.29
  250.8 0.0 copy-done.1
  250.8 0.0 copy-start
  250.8 1.3 copy.30
  252.2 1.0 copy-done
  253.2 1.3 copy.31
Async XLA Ops:
  246.9 4.0 %copy-start.1 = (f32[1024,512]{1,0:T(8,128)S(1)}, f32[1024,512]{1,0:T(8,128)}, u32[]{:S(2)}) copy-start(f32[1024,512]{1,0:T(8,128)} %get-tuple-element.10) | copy-start | bytes 6291460
  250.8 2.3 copy-start

commit v3 on v2

v3 whole, which is shorter than its diff:
```python
import jax
import jax.numpy as jnp
from jax import lax
from jax.experimental import pallas as pl
from jax.experimental.pallas import tpu as pltpu
from jax.sharding import PartitionSpec as P

QB = 128
BF = jnp.bfloat16
F32 = jnp.float32
MESH = pl.DeviceIdType.MESH

beta_first = 0.9
beta_second = 0.95
adam_eps = 1e-08
learn_rate = 0.003
decay_rate = 0.1
step_count = 20
fix_first = 1.0 - beta_first**step_count
fix_second = 1.0 - beta_second**step_count

VMEM_LIMIT = 58 * 1024 * 1024

T, SC, D1, F1, S1, D2, F2, S2, H1, H2, O, Y1, Y2, W, CX, CU = range(16)
KINDS = CU + 8


def transposed_dot(a, b):
    return lax.dot_general(a, b, (((0,), (0,)), ((), ())), preferred_element_type=F32)


def step_kernel(
    old_hbm,
    holder_hbm,
    gate_scale_hbm,
    up_scale_hbm,
    route_hbm,
    weight_hbm,
    tok_hbm,
    cot_hbm,
    scale_hbm,
    gate_hbm,
    up_hbm,
    down_hbm,
    first_hbm,
    second_hbm,
    grad_hbm,
    down_new_hbm,
    first_new,
    second_new,
    out_recv,
    pick_hbm,
    wide_hbm,
    old_ref,
    holder_ref,
    gate_scale_ref,
    up_scale_ref,
    route_ref,
    weight_ref,
    tok_ref,
    scale_ref,
    giver_ref,
    lanes_ref,
    tok_send,
    tok_recv,
    note_send,
    note_all,
    down_mid,
    first_send,
    first_mid,
    second_send,
    second_mid,
    cot_all,
    back_ref,
    down_out,
    down_new,
    first_out,
    second_out,
    hid_send,
    hid_mid,
    hid_out,
    hid_new,
    out_send,
    rows_all,
    weights_all,
    gate_v,
    up_v,
    hidden_all,
    grad_ref,
    pick_ref,
    wide_ref,
    send_sem,
    recv_sem,
    local_sem,
    load_sem,
):
    number = lax.axis_size("expert")
    parts = lax.axis_size("dp")
    cores = weights_all.shape[0]
    columns, depth = cot_all.shape[:2]
    e = lax.axis_index("expert")
    d = lax.axis_index("dp")
    core = lax.rem(d, cores)
    z = e // columns
    x = lax.rem(e, columns)
    tokens, width = tok_ref.shape
    slots = tok_send.shape[1]
    total = number * slots
    half = number // cores
    half_rows = half * slots
    hidden_part = gate_v.shape[1]

    def remote(src, dst, kind, target):
        return pltpu.make_async_remote_copy(
            src_ref=src,
            dst_ref=dst,
            send_sem=send_sem.at[kind],
            recv_sem=recv_sem.at[kind],
            device_id=target,
            device_id_type=MESH,
        )

    load_gate = pltpu.make_async_copy(gate_hbm, gate_v, load_sem.at[0])
    load_up = pltpu.make_async_copy(up_hbm, up_v, load_sem.at[1])
    load_first = pltpu.make_async_copy(first_hbm, grad_ref, load_sem.at[2])
    load_second = pltpu.make_async_copy(second_hbm, grad_ref, load_sem.at[3])
    small = [
        pltpu.make_async_copy(src, dst, load_sem.at[4 + i])
        for i, (src, dst) in enumerate(
            [
                (route_hbm, route_ref),
                (old_hbm, old_ref),
                (tok_hbm, tok_ref),
                (cot_hbm, cot_all.at[x, z]),
                (weight_hbm, weight_ref),
                (holder_hbm, holder_ref),
                (gate_scale_hbm, gate_scale_ref),
                (up_scale_hbm, up_scale_ref),
                (scale_hbm, scale_ref),
            ]
        )
    ]
    for load in small:
        load.start()
    load_gate.start()
    load_up.start()
    load_first.start()

    barrier = pltpu.get_barrier_semaphore()

    def greet_expert(k, carry):
        pl.semaphore_signal(
            barrier, inc=1, device_id=(lax.rem(e + k, number), d), device_id_type=MESH
        )
        return carry

    def greet_dp(k, carry):
        pl.semaphore_signal(
            barrier, inc=1, device_id=(e, lax.rem(d + k, parts)), device_id_type=MESH
        )
        return carry

    lax.fori_loop(1, number, greet_expert, 0)
    lax.fori_loop(1, parts, greet_dp, 0)

    i = lax.broadcasted_iota(jnp.int32, (tokens, tokens), 0)
    j = lax.broadcasted_iota(jnp.int32, (tokens, tokens), 1)
    earlier = (i < j).astype(BF)
    row = lax.broadcasted_iota(jnp.int32, (total, number), 0)
    holder = lax.broadcasted_iota(jnp.int32, (total, number), 1)
    spread = jnp.logical_and(row >= holder * slots, row < (holder + 1) * slots).astype(BF)
    place = lax.rem(lax.broadcasted_iota(jnp.int32, (total, tokens), 0), slots).astype(F32)
    label = lax.broadcasted_iota(jnp.int32, (number, tokens), 0)

    def ranks(hit):
        rank = jnp.dot(hit.astype(BF), earlier, preferred_element_type=F32)
        return jnp.where(hit > 0.0, rank, -1.0)

    def slot_hits(rank):
        return jnp.dot(spread, rank.astype(BF), preferred_element_type=F32) == place

    def experts_of(value_of):
        named = jnp.zeros((number, tokens), jnp.int32)
        for h in range(number):
            named = jnp.where(label == h, value_of(h), named)
        return named

    small[0].wait()
    small[1].wait()
    routes = route_ref[...]
    expert_before = experts_of(lambda h: old_ref[h])
    hit_before = jnp.zeros((number, tokens), F32)
    for k in range(routes.shape[0]):
        hit_before += (routes[k : k + 1, :] == expert_before).astype(F32)
    pick = slot_hits(ranks(hit_before)).astype(BF)
    small[2].wait()
    rows = jnp.dot(pick, tok_ref[...], preferred_element_type=F32)
    tok_send[...] = rows.astype(BF).reshape(tok_send.shape)

    pl.semaphore_wait(barrier, number - 1 + parts - 1)

    def send_all(src, dst, kind):
        def body(k, carry):
            t = lax.rem(e + k, number)
            remote(src.at[t], dst.at[e], kind, (t, d)).start()
            return carry

        lax.fori_loop(1, number, body, 0)
        pltpu.make_async_copy(src.at[e], dst.at[e], local_sem.at[kind]).start()

    def wait_all(src, dst, kind):
        rest = dst.at[pl.ds(0, number - 1)]
        remote(rest, rest, kind, (lax.rem(e + 1, number), d)).wait_recv()
        pltpu.make_async_copy(src.at[e], dst.at[e], local_sem.at[kind]).wait()

    def sent_all(dst, kind):
        rest = dst.at[pl.ds(0, number - 1)]
        remote(rest, rest, kind, (lax.rem(e + 1, number), d)).wait_send()

    def reorder(src, dst):
        def body(k, carry):
            dst[k] = src[giver_ref[k]]
            return carry

        lax.fori_loop(0, number, body, 0)

    send_all(tok_send, tok_recv, T)

    def ring(step, source, lines):
        above = (lax.rem(z + 1, depth) * columns + x, d)
        below = (lax.rem(z + depth - 1, depth) * columns + x, d)
        from_below = cot_all.at[x, lax.rem(z + depth - source, depth)]
        from_above = cot_all.at[x, lax.rem(z + source, depth)]
        if lines is not None:
            from_below = from_below.at[pl.ds(0, lines)]
            from_above = from_above.at[pl.ds(lines, lines)]
        up = remote(from_below, from_below, CU + 2 * step, above)
        down = remote(from_above, from_above, CU + 2 * step + 1, below)
        return up, down

    small[3].wait()
    rings = [ring(0, 0, None)]
    for copy in rings[0]:
        copy.start()

    load_gate.wait()
    load_up.wait()
    small[6].wait()
    small[7].wait()

    def dequantize(r, carry):
        lines = pl.ds(pl.multiple_of(r * QB, QB), QB)
        gate = (gate_v[lines, :].astype(F32) * gate_scale_ref[r]).astype(BF)
        up = (up_v[lines, :].astype(F32) * up_scale_ref[r]).astype(BF)
        weights_all[core, lines, :] = jnp.concatenate([gate, up], axis=1)
        return carry

    lax.fori_loop(0, gate_v.shape[0] // QB, dequantize, 0)
    sibling = (e, d + 1 - 2 * core)
    weights_copy = remote(weights_all.at[core], weights_all.at[core], W, sibling)
    weights_copy.start()

    for load in small[4:6] + small[8:]:
        load.wait()

    def forward(step, lines=None):
        for copy in rings[step - 1]:
            copy.wait_recv()
        rings.append(ring(step, step, lines))
        for copy in rings[step]:
            copy.start()

    forward(1)

    def find(h, carry):
        giver = jnp.int32(0)
        for g in range(number):
            giver = jnp.where(holder_ref[g] == h, g, giver)
        giver_ref[h] = giver
        return carry

    lax.fori_loop(0, number, find, 0)
    expert_after = experts_of(lambda h: old_ref[giver_ref[h]])
    hit_after = jnp.zeros((number, tokens), F32)
    weight_after = jnp.zeros((number, tokens), F32)
    for k in range(routes.shape[0]):
        match = routes[k : k + 1, :] == expert_after
        hit_after += match.astype(F32)
        weight_after += jnp.where(match, weight_ref[k : k + 1, :], 0.0)
    rank_after = ranks(hit_after)
    lanes_ref[...] = jnp.zeros_like(lanes_ref)
    lanes_ref[0, :, :tokens] = rank_after
    lanes_ref[1, :, :tokens] = weight_after
    note_rows, note_lanes = scale_ref.shape
    line = lax.broadcasted_iota(jnp.int32, (note_rows, note_lanes), 0)
    lane = lax.broadcasted_iota(jnp.int32, (note_rows, note_lanes), 1)
    for h in range(number):
        rank_row = jnp.broadcast_to(lanes_ref[0, h : h + 1, :], scale_ref.shape)
        weight_row = jnp.broadcast_to(lanes_ref[1, h : h + 1, :], scale_ref.shape)
        note = jnp.where(line == 0, rank_row, jnp.where(line == 1, weight_row, 0.0))
        note_send[h] = jnp.where(lane < tokens, note, scale_ref[...])
    send_all(note_send, note_all, SC)

    forward(2)
    load_first.wait()
    first_send[...] = grad_ref[...].astype(BF).reshape(first_send.shape)
    load_second.start()

    sent_all(tok_recv, T)
    send_all(down_hbm, down_mid, D1)

    hit_slots = slot_hits(rank_after)
    rest = weight_after
    for p in range(3):
        piece = rest.astype(BF)
        rest = rest - piece.astype(F32)
        wide = jnp.dot(spread, piece, preferred_element_type=F32)
        pick_ref[p] = jnp.where(hit_slots, wide, 0.0).astype(BF)
    forward(3, tokens // 2)
    load_second.wait()
    second_send[...] = grad_ref[...].astype(BF).reshape(second_send.shape)

    wait_all(tok_send, tok_recv, T)

    def send_rows(k, carry):
        t = lax.rem(d + k, parts)
        src = tok_recv.at[pl.ds(lax.rem(t, cores) * half, half)]
        remote(src, rows_all.at[d], Y1, (e, t)).start()
        return carry

    lax.fori_loop(1, parts, send_rows, 0)
    own_rows = pltpu.make_async_copy(
        tok_recv.at[pl.ds(core * half, half)], rows_all.at[d], local_sem.at[Y1]
    )
    own_rows.start()
    for copy in rings[3]:
        copy.wait_recv()

    def send_column(k, carry):
        t = (z * columns + lax.rem(x + k, columns), d)
        remote(cot_all.at[x], cot_all.at[x], CX, t).start()
        return carry

    lax.fori_loop(1, columns, send_column, 0)
    send_all(first_send, first_mid, F1)
    send_all(second_send, second_mid, S1)

    wait_all(down_hbm, down_mid, D1)
    reorder(down_mid, down_out)
    send_all(down_out, down_new, D2)

    own_rows.wait()
    weights_copy.wait()
    others = rows_all.at[pl.ds(0, parts - 1)]
    remote(others, others, Y1, sibling).wait()
    for c in range(cores):
        value = jnp.zeros((half_rows, 2 * hidden_part), F32)
        for k in range(parts):
            value += jnp.dot(
                rows_all[k].reshape(half_rows, width),
                weights_all[c, k * width : (k + 1) * width, :],
                preferred_element_type=F32,
            )
        gate = value[:, :hidden_part]
        up = value[:, hidden_part:]
        act = (gate / (1.0 + jnp.exp(-gate)) * up).astype(BF)
        hid_send[:, :, c * hidden_part : (c + 1) * hidden_part] = act.reshape(
            number, half_rows // number, hidden_part
        )
    send_all(hid_send, hid_mid, H1)

    wait_all(first_send, first_mid, F1)
    reorder(first_mid, first_out)
    send_all(first_out, first_new, F2)

    wait_all(hid_send, hid_mid, H1)
    reorder(hid_mid, hid_out)
    send_all(hid_out, hid_new, H2)

    wait_all(second_send, second_mid, S1)
    reorder(second_mid, second_out)
    send_all(second_out, second_new, S2)

    wait_all(hid_out, hid_new, H2)

    def send_hidden(k, carry):
        remote(hid_new, hidden_all.at[d], Y2, (e, lax.rem(d + k, parts))).start()
        return carry

    lax.fori_loop(1, parts, send_hidden, 0)
    own_hidden = pltpu.make_async_copy(hid_new, hidden_all.at[d], local_sem.at[Y2])
    own_hidden.start()

    wait_all(note_send, note_all, SC)
    wait_all(down_out, down_new, D2)
    save_down = pltpu.make_async_copy(down_new, down_new_hbm, load_sem.at[0])
    save_down.start()
    save_pick = pltpu.make_async_copy(pick_ref, pick_hbm, load_sem.at[1])
    save_pick.start()
    scale = note_all[giver_ref[e]]
    scale_wide = jnp.concatenate(
        [
            jnp.broadcast_to(scale[:, tokens + c : tokens + c + 1], (scale.shape[0], QB))
            for c in range(width // QB)
        ],
        axis=1,
    )
    wide_ref[...] = scale_wide
    save_wide = pltpu.make_async_copy(wide_ref, wide_hbm, load_sem.at[2])
    save_wide.start()
    pieces = QB // down_new.shape[1]

    def weight_rows(r):
        quant = down_new[r * pieces : (r + 1) * pieces].reshape(QB, width)
        return (quant.astype(F32) * scale_wide[r : r + 1, :]).astype(BF)

    own_hidden.wait()
    others = hidden_all.at[pl.ds(0, parts - 1)]
    remote(others, others, Y2, sibling).wait()
    pair = cores * hidden_part
    for c in range(cores):
        value = jnp.zeros((half_rows, width), F32)
        for y in range(parts // cores):
            down_w = jnp.concatenate(
                [weight_rows(y * pair // QB + r) for r in range(pair // QB)], axis=0
            )
            value += jnp.dot(
                hidden_all[y * cores + c].reshape(half_rows, pair),
                down_w,
                preferred_element_type=F32,
            )
        out_send[c * half : (c + 1) * half] = value.astype(BF).reshape(half, slots, width)
    send_all(out_send, out_recv, O)

    others = cot_all.at[pl.ds(0, columns - 1)]
    remote(others, others, CX, sibling).wait()
    for s in range(number):
        slot = lax.broadcasted_iota(jnp.int32, (slots, tokens), 0).astype(F32)
        hit = note_all[s, 0:1, :tokens] == slot
        weight = jnp.sum(jnp.where(hit, note_all[s, 1:2, :tokens], 0.0), axis=1, keepdims=True)
        block = cot_all[s % columns, s // columns]
        picked = jnp.dot(hit.astype(BF), block, preferred_element_type=F32)
        back_ref[s] = (weight * picked).astype(BF)

    for y in range(parts // cores):
        value = jnp.zeros((pair, width), F32)
        for c in range(cores):
            value += transposed_dot(
                hidden_all[y * cores + c].reshape(half_rows, pair),
                back_ref[c * half : (c + 1) * half].reshape(half_rows, width),
            )
        grad_ref[y * pair : (y + 1) * pair, :] = value
    save_grad = pltpu.make_async_copy(grad_ref, grad_hbm, load_sem.at[3])
    save_grad.start()

    for pair_of_copies in rings:
        for copy in pair_of_copies:
            copy.wait_send()
    for dst, kind in (
        (note_all, SC),
        (down_mid, D1),
        (first_mid, F1),
        (second_mid, S1),
        (down_new, D2),
        (first_new, F2),
        (second_new, S2),
        (hid_mid, H1),
        (hid_new, H2),
        (out_recv, O),
    ):
        sent_all(dst, kind)
    wait_all(first_out, first_new, F2)
    wait_all(second_out, second_new, S2)
    wait_all(out_send, out_recv, O)
    for save in (save_down, save_pick, save_wide, save_grad):
        save.wait()


def finish_kernel(
    grad_ref,
    down_ref,
    first_in,
    second_in,
    wide_ref,
    pick_ref,
    rows_ref,
    mixed_ref,
    fresh_ref,
    first_ref,
    second_ref,
):
    k = pl.program_id(0)
    tall, width = grad_ref.shape

    @pl.when(k == 0)
    def _():
        rows = rows_ref[...].reshape(-1, width)
        value = transposed_dot(pick_ref[0], rows)
        value += transposed_dot(pick_ref[1], rows)
        value += transposed_dot(pick_ref[2], rows)
        mixed_ref[...] = value.astype(BF)

    grad = grad_ref[...]
    quant = down_ref[...].reshape(tall, width).astype(F32)
    lines = tall // QB
    master = jnp.concatenate(
        [
            quant[r * QB : (r + 1) * QB, :] * wide_ref[pl.ds(k * lines + r, 1), :]
            for r in range(lines)
        ],
        axis=0,
    )
    first = first_in[...].reshape(tall, width).astype(F32)
    second = second_in[...].reshape(tall, width).astype(F32)
    first = beta_first * first + (1.0 - beta_first) * grad
    second = beta_second * second + (1.0 - beta_second) * grad * grad
    update = first / fix_first / (jnp.sqrt(second / fix_second) + adam_eps)
    fresh_ref[0] = (master - learn_rate * (update + decay_rate * master)).astype(BF)
    first_ref[0] = first
    second_ref[0] = second


def finish(grad, down_new, first_new, second_new, wide, pick, out_rows):
    hidden_total, width = grad.shape
    number, piece_rows, _ = down_new.shape
    tokens = pick.shape[2]
    steps = 4
    tall = hidden_total // steps
    state = pl.BlockSpec((number // steps, piece_rows, width), lambda k: (k, 0, 0))
    block = pl.BlockSpec((1, tall, width), lambda k: (0, k, 0))
    return pl.pallas_call(
        finish_kernel,
        grid=(steps,),
        in_specs=[
            pl.BlockSpec((tall, width), lambda k: (k, 0)),
            state,
            state,
            state,
            pl.BlockSpec(wide.shape, lambda k: (0, 0)),
            pl.BlockSpec(pick.shape, lambda k: (0, 0, 0)),
            pl.BlockSpec(out_rows.shape, lambda k: (0, 0, 0)),
        ],
        out_specs=[pl.BlockSpec((tokens, width), lambda k: (0, 0)), block, block, block],
        out_shape=[
            jax.ShapeDtypeStruct((tokens, width), BF),
            jax.ShapeDtypeStruct((1, hidden_total, width), BF),
            jax.ShapeDtypeStruct((1, hidden_total, width), F32),
            jax.ShapeDtypeStruct((1, hidden_total, width), F32),
        ],
        compiler_params=pltpu.CompilerParams(vmem_limit_bytes=VMEM_LIMIT),
        name="finish",
    )(grad, down_new, first_new, second_new, wide, pick, out_rows)


def per_device(
    tokens,
    route_weight,
    route_expert,
    cotangent,
    gate_quant,
    up_quant,
    gate_scale,
    up_scale,
    down_quant,
    down_scale,
    first_moment,
    second_moment,
    old_expert,
    new_holder,
):
    number = lax.axis_size("expert")
    parts = lax.axis_size("dp")
    cores = 2
    columns = 4
    tok_rows, top_count = route_expert.shape
    width = cotangent.shape[1]
    slots = min(tok_rows, tok_rows * top_count // number * 4 // 3)
    model_width, hidden_part = gate_quant.shape[1:]
    hidden_total = down_quant.shape[1]
    piece_rows = hidden_total // number
    scale_cols = down_scale.shape[2]
    scale = jnp.pad(down_scale[0], ((0, 0), (tok_rows, QB - tok_rows - scale_cols)))

    hbm = pl.BlockSpec(memory_space=pl.ANY)
    state_shape = (number, piece_rows, width)
    row_shape = (number, slots, width)
    pick_shape = (3, number * slots, tok_rows)
    wide_shape = (scale.shape[0], width)
    half_rows = number * slots // cores
    state = pltpu.VMEM(state_shape, BF)
    rows = pltpu.VMEM(row_shape, BF)
    note = pltpu.VMEM((number,) + scale.shape, F32)
    hid_shape = (number, half_rows // number, cores * hidden_part)
    hid = pltpu.VMEM(hid_shape, BF)
    parts_out = pl.pallas_call(
        step_kernel,
        in_specs=[hbm] * 14,
        out_specs=[hbm] * 7,
        out_shape=[
            jax.ShapeDtypeStruct((hidden_total, width), F32),
            jax.ShapeDtypeStruct(state_shape, BF),
            jax.ShapeDtypeStruct(state_shape, BF),
            jax.ShapeDtypeStruct(state_shape, BF),
            jax.ShapeDtypeStruct(row_shape, BF),
            jax.ShapeDtypeStruct(pick_shape, BF),
            jax.ShapeDtypeStruct(wide_shape, F32),
        ],
        scratch_shapes=[
            pltpu.SMEM((number,), jnp.int32),
            pltpu.SMEM((number,), jnp.int32),
            pltpu.SMEM((model_width // QB,), F32),
            pltpu.SMEM((model_width // QB,), F32),
            pltpu.VMEM((top_count, tok_rows), jnp.int32),
            pltpu.VMEM((top_count, tok_rows), F32),
            pltpu.VMEM((tok_rows, width), BF),
            pltpu.VMEM(scale.shape, F32),
            pltpu.SMEM((number,), jnp.int32),
            pltpu.VMEM((2, number, QB), F32),
            rows,
            rows,
            note,
            note,
            state,
            state,
            state,
            state,
            state,
            pltpu.VMEM((columns, number // columns, tok_rows, width), BF),
            rows,
            state,
            state,
            state,
            state,
            hid,
            hid,
            hid,
            hid,
            rows,
            pltpu.VMEM((parts, number // cores, slots, width), BF),
            pltpu.VMEM((cores, model_width, 2 * hidden_part), BF),
            pltpu.VMEM((model_width, hidden_part), BF),
            pltpu.VMEM((model_width, hidden_part), BF),
            pltpu.VMEM((parts,) + hid_shape, BF),
            pltpu.VMEM((hidden_total, width), F32),
            pltpu.VMEM(pick_shape, BF),
            pltpu.VMEM(wide_shape, F32),
            pltpu.SemaphoreType.DMA((KINDS,)),
            pltpu.SemaphoreType.DMA((KINDS,)),
            pltpu.SemaphoreType.DMA((KINDS,)),
            pltpu.SemaphoreType.DMA((13,)),
        ],
        compiler_params=pltpu.CompilerParams(
            collective_id=0, has_side_effects=True, vmem_limit_bytes=VMEM_LIMIT
        ),
        name="step",
    )(
        old_expert,
        new_holder,
        gate_scale.reshape(-1),
        up_scale.reshape(-1),
        route_expert.T,
        route_weight.T,
        tokens,
        cotangent,
        scale,
        gate_quant[0],
        up_quant[0],
        down_quant.reshape(state_shape),
        first_moment[0],
        second_moment[0],
    )
    grad, down_new, first_new, second_new, out_rows, pick, wide = parts_out
    return tuple(finish(grad, down_new, first_new, second_new, wide, pick, out_rows))


def solution(mesh):
    in_specs = (
        P("expert", "dp"),
        P("expert", None),
        P("expert", None),
        P("expert", "dp"),
        P("expert", None, "dp"),
        P("expert", None, "dp"),
        P("expert", None, "dp"),
        P("expert", None, "dp"),
        P("expert", None, "dp"),
        P("expert", None, "dp"),
        P("expert", None, "dp"),
        P("expert", None, "dp"),
        P(),
        P(),
    )
    out_specs = (
        P("expert", "dp"),
        P("expert", None, "dp"),
        P("expert", None, "dp"),
        P("expert", None, "dp"),
    )
    return jax.shard_map(
        per_device, mesh=mesh, in_specs=in_specs, out_specs=out_specs, check_vma=False
    )
```

time: 255 us -> 234 us (0.918)
  local copies, waits for them, and re-layouts: 11.8 us -> 1.42 us
  Pallas kernels: 239 us -> 232 us
  other arithmetic: 2.65 us -> 0 us
    unnamed x10 -> x0, local copies, waits for them, and re-layouts: 10.4 us -> none
    pallas_call x1 -> x2, Pallas kernels: 239 us -> 232 us  [the longest x1 224 us: per_device(): pl.pallas_call(step_kernel, in_specs=[hbm] * 14, out_specs=[hbm] * 7, out...]
    reduce_sum x2 -> x0, other arithmetic: 2.65 us -> none  [the longest x1 1.37 us: per_device(): my_giver = jnp.sum(jnp.where(new_holder == me, labels, 0)).reshape(1)]
where the time goes in v3:
time: 234 us
  Pallas kernels  232 us (99%)
    pallas_call x1, Pallas kernels, per_device(): pl.pallas_call(step_kernel, in_specs=[hbm] * 14, out_specs=[hbm] * 7, out...  224 us
    pallas_call x1, Pallas kernels, finish(): pl.pallas_call(finish_kernel, grid=(steps,), in_specs=[pl.BlockSpec((tall...  7.3 us

profile of v3, /device:TPU:1, one launch (start us, length us, event | category | flops | bytes accessed | tf_op | source)
XLA Modules:
  0.0 233.8 jit_solution(13133512866641294274)
XLA Ops:
  0.6 0.8 copy.18
  1.4 0.7 pad.4.scale_hbm
  2.1 224.4 %step.1 = (f32[1024,512]{1,0:T(8,128)}, bf16[32,32,512]{2,1,0:T(8,128)(2,1)}, bf16[32,32,512]{2,1,0:T(8,128)(2,1)}, bf16[32,32,512]{2,1,0:T(8,128)(2,1)}, bf16[3...) custom-call(s32[32]{0:T(128)} %old_hbm.1, s32[32]{0:T(128)} %holder_hbm.1, f32[32]{0:T(128)} %bitcast.18, ...), custom_call_target="tpu_custom_call" | custom-call | tf_op jit(solution)/shard_map/step/pallas_call | solution.py:595
  226.5 7.3 %finish.1 = (bf16[96,512]{1,0:T(8,128)(2,1)}, bf16[1,1024,512]{2,1,0:T(8,128)(2,1)}, f32[1,1024,512]{2,1,0:T(8,128)}, f32[1,1024,512]{2,1,0:T(8,128)}) custom-call(f32[1024,512]{1,0:T(8,128)} %get-tuple-element.11.grad_ref, bf16[32,32,512]{2,1,0:T(8,128)(2,1)} %get-tuple-element.12.down_ref, bf16[32,32,512]{2,1,0:T(8,128)(2,1)} %get-tuple-element.13.first_in, ...), custom_call_target="tpu_custom_call" | custom-call | tf_op jit(solution)/shard_map/finish/pallas_call | solution.py:531

commit v4 on v3

--- a/solution.py
+++ b/solution.py
@@ -21,8 +21,16 @@
 
 VMEM_LIMIT = 58 * 1024 * 1024
 
-T, SC, D1, F1, S1, D2, F2, S2, H1, H2, O, Y1, Y2, W, CX, CU = range(16)
-KINDS = CU + 8
+SC, D1, F1, S1, D2, F2, S2, H1, H2, O, W, CX, TX, YS, YFU, YFD, Y2, Y3 = range(18)
+YU = 18
+YD = 20
+TU = 22
+CU = 30
+TF = 38
+CF = 40
+TB = 42
+CB = 43
+KINDS = 44
 
 
 def transposed_dot(a, b):
@@ -57,11 +65,10 @@
     up_scale_ref,
     route_ref,
     weight_ref,
-    tok_ref,
     scale_ref,
     giver_ref,
     lanes_ref,
-    tok_send,
+    tok_all,
     tok_recv,
     note_send,
     note_all,
@@ -103,8 +110,10 @@
     core = lax.rem(d, cores)
     z = e // columns
     x = lax.rem(e, columns)
-    tokens, width = tok_ref.shape
-    slots = tok_send.shape[1]
+    chip = d // cores
+    chips = parts // cores
+    tokens, width = tok_all.shape[2:]
+    slots = tok_recv.shape[1]
     total = number * slots
     half = number // cores
     half_rows = half * slots
@@ -130,7 +139,7 @@
             [
                 (route_hbm, route_ref),
                 (old_hbm, old_ref),
-                (tok_hbm, tok_ref),
+                (tok_hbm, tok_all.at[x, z]),
                 (cot_hbm, cot_all.at[x, z]),
                 (weight_hbm, weight_ref),
                 (holder_hbm, holder_ref),
@@ -163,49 +172,16 @@
     lax.fori_loop(1, number, greet_expert, 0)
     lax.fori_loop(1, parts, greet_dp, 0)
 
-    i = lax.broadcasted_iota(jnp.int32, (tokens, tokens), 0)
-    j = lax.broadcasted_iota(jnp.int32, (tokens, tokens), 1)
-    earlier = (i < j).astype(BF)
-    row = lax.broadcasted_iota(jnp.int32, (total, number), 0)
-    holder = lax.broadcasted_iota(jnp.int32, (total, number), 1)
-    spread = jnp.logical_and(row >= holder * slots, row < (holder + 1) * slots).astype(BF)
-    place = lax.rem(lax.broadcasted_iota(jnp.int32, (total, tokens), 0), slots).astype(F32)
-    label = lax.broadcasted_iota(jnp.int32, (number, tokens), 0)
-
-    def ranks(hit):
-        rank = jnp.dot(hit.astype(BF), earlier, preferred_element_type=F32)
-        return jnp.where(hit > 0.0, rank, -1.0)
-
-    def slot_hits(rank):
-        return jnp.dot(spread, rank.astype(BF), preferred_element_type=F32) == place
-
-    def experts_of(value_of):
-        named = jnp.zeros((number, tokens), jnp.int32)
-        for h in range(number):
-            named = jnp.where(label == h, value_of(h), named)
-        return named
-
-    small[0].wait()
-    small[1].wait()
-    routes = route_ref[...]
-    expert_before = experts_of(lambda h: old_ref[h])
-    hit_before = jnp.zeros((number, tokens), F32)
-    for k in range(routes.shape[0]):
-        hit_before += (routes[k : k + 1, :] == expert_before).astype(F32)
-    pick = slot_hits(ranks(hit_before)).astype(BF)
-    small[2].wait()
-    rows = jnp.dot(pick, tok_ref[...], preferred_element_type=F32)
-    tok_send[...] = rows.astype(BF).reshape(tok_send.shape)
-
-    pl.semaphore_wait(barrier, number - 1 + parts - 1)
-
-    def send_all(src, dst, kind):
+    def send_part(src, dst, kind, first, last):
         def body(k, carry):
             t = lax.rem(e + k, number)
             remote(src.at[t], dst.at[e], kind, (t, d)).start()
             return carry
 
-        lax.fori_loop(1, number, body, 0)
+        lax.fori_loop(first, last, body, 0)
+
+    def send_all(src, dst, kind):
+        send_part(src, dst, kind, 1, number)
         pltpu.make_async_copy(src.at[e], dst.at[e], local_sem.at[kind]).start()
 
     def wait_all(src, dst, kind):
@@ -224,66 +200,86 @@
 
         lax.fori_loop(0, number, body, 0)
 
-    send_all(tok_send, tok_recv, T)
-
-    def ring(step, source, lines):
+    def ring(table, base, step):
         above = (lax.rem(z + 1, depth) * columns + x, d)
         below = (lax.rem(z + depth - 1, depth) * columns + x, d)
-        from_below = cot_all.at[x, lax.rem(z + depth - source, depth)]
-        from_above = cot_all.at[x, lax.rem(z + source, depth)]
-        if lines is not None:
+        from_below = table.at[x, lax.rem(z + depth - step, depth)]
+        from_above = table.at[x, lax.rem(z + step, depth)]
+        if step == depth // 2 - 1:
+            lines = tokens // 2
             from_below = from_below.at[pl.ds(0, lines)]
             from_above = from_above.at[pl.ds(lines, lines)]
-        up = remote(from_below, from_below, CU + 2 * step, above)
-        down = remote(from_above, from_above, CU + 2 * step + 1, below)
+        up = remote(from_below, from_below, base + 2 * step, above)
+        down = remote(from_above, from_above, base + 2 * step + 1, below)
         return up, down
 
-    small[3].wait()
-    rings = [ring(0, 0, None)]
-    for copy in rings[0]:
-        copy.start()
-
-    load_gate.wait()
-    load_up.wait()
-    small[6].wait()
-    small[7].wait()
-
-    def dequantize(r, carry):
-        lines = pl.ds(pl.multiple_of(r * QB, QB), QB)
-        gate = (gate_v[lines, :].astype(F32) * gate_scale_ref[r]).astype(BF)
-        up = (up_v[lines, :].astype(F32) * up_scale_ref[r]).astype(BF)
-        weights_all[core, lines, :] = jnp.concatenate([gate, up], axis=1)
-        return carry
-
-    lax.fori_loop(0, gate_v.shape[0] // QB, dequantize, 0)
     sibling = (e, d + 1 - 2 * core)
-    weights_copy = remote(weights_all.at[core], weights_all.at[core], W, sibling)
-    weights_copy.start()
-
-    for load in small[4:6] + small[8:]:
-        load.wait()
-
-    def forward(step, lines=None):
-        for copy in rings[step - 1]:
+    right = (z * columns + lax.rem(x + 1, columns), d)
+    left = (z * columns + lax.rem(x + columns - 1, columns), d)
+    right_x, left_x = lax.rem(x + 1, columns), lax.rem(x + columns - 1, columns)
+
+    def along_x(block, kinds):
+        remote(block, block, kinds[0], right).start()
+        remote(block, block, kinds[1], left).start()
+
+    def pass_on(table, kinds, onward):
+        copies = []
+        for kind, k, source, low, target in (
+            (kinds[0], onward, left_x, 0, right),
+            (kinds[1], onward + 1, right_x, depth // 2, left),
+        ):
+            column = table.at[source]
+            remote(column, column, kind, sibling).wait_recv()
+            part = table.at[source, pl.ds(low, depth // 2)]
+            copy = remote(part, part, k, target)
+            copy.start()
+            copies.append(copy)
+        return copies
+
+    token_rings = [ring(tok_all, TU, step) for step in range(depth // 2)]
+    cot_rings = [ring(cot_all, CU, step) for step in range(depth // 2)]
+
+    def start(copies):
+        for copy in copies:
+            copy.start()
+
+    def arrive(copies):
+        for copy in copies:
             copy.wait_recv()
-        rings.append(ring(step, step, lines))
-        for copy in rings[step]:
-            copy.start()
-
-    forward(1)
-
-    def find(h, carry):
-        giver = jnp.int32(0)
-        for g in range(number):
-            giver = jnp.where(holder_ref[g] == h, g, giver)
-        giver_ref[h] = giver
-        return carry
-
-    lax.fori_loop(0, number, find, 0)
-    expert_after = experts_of(lambda h: old_ref[giver_ref[h]])
+
+    small[2].wait()
+    pl.semaphore_wait(barrier, number - 1 + parts - 1)
+
+    portion = number // 4
+    start(token_rings[0])
+    along_x(tok_all.at[x, z], (TX, TB))
+    send_part(down_hbm, down_mid, D1, 1, portion)
+
+    i = lax.broadcasted_iota(jnp.int32, (tokens, tokens), 0)
+    j = lax.broadcasted_iota(jnp.int32, (tokens, tokens), 1)
+    earlier = (i < j).astype(BF)
+    label = lax.broadcasted_iota(jnp.int32, (number, tokens), 0)
+
+    def ranks(hit):
+        rank = jnp.dot(hit.astype(BF), earlier, preferred_element_type=F32)
+        return jnp.where(hit > 0.0, rank, -1.0)
+
+    small[0].wait()
+    small[1].wait()
+    small[4].wait()
+    small[5].wait()
+    small[8].wait()
+    expert_before = jnp.zeros((number, tokens), jnp.int32)
+    expert_after = jnp.zeros((number, tokens), jnp.int32)
+    for h in range(number):
+        expert_before = jnp.where(label == h, old_ref[h], expert_before)
+        expert_after = jnp.where(label == holder_ref[h], old_ref[h], expert_after)
+    routes = route_ref[...]
+    hit_before = jnp.zeros((number, tokens), F32)
     hit_after = jnp.zeros((number, tokens), F32)
     weight_after = jnp.zeros((number, tokens), F32)
     for k in range(routes.shape[0]):
+        hit_before += (routes[k : k + 1, :] == expert_before).astype(F32)
         match = routes[k : k + 1, :] == expert_after
         hit_after += match.astype(F32)
         weight_after += jnp.where(match, weight_ref[k : k + 1, :], 0.0)
@@ -291,76 +287,157 @@
     lanes_ref[...] = jnp.zeros_like(lanes_ref)
     lanes_ref[0, :, :tokens] = rank_after
     lanes_ref[1, :, :tokens] = weight_after
-    note_rows, note_lanes = scale_ref.shape
-    line = lax.broadcasted_iota(jnp.int32, (note_rows, note_lanes), 0)
-    lane = lax.broadcasted_iota(jnp.int32, (note_rows, note_lanes), 1)
+    lanes_ref[2, :, :tokens] = ranks(hit_before)
+    note_shape = note_send.shape[1:]
+    line = lax.broadcasted_iota(jnp.int32, note_shape, 0)
+    lane = lax.broadcasted_iota(jnp.int32, note_shape, 1)
     for h in range(number):
-        rank_row = jnp.broadcast_to(lanes_ref[0, h : h + 1, :], scale_ref.shape)
-        weight_row = jnp.broadcast_to(lanes_ref[1, h : h + 1, :], scale_ref.shape)
-        note = jnp.where(line == 0, rank_row, jnp.where(line == 1, weight_row, 0.0))
+        note = jnp.zeros(note_shape, F32)
+        for r in range(3):
+            spread_row = jnp.broadcast_to(lanes_ref[r, h : h + 1, :], note_shape)
+            note = jnp.where(line == r, spread_row, note)
         note_send[h] = jnp.where(lane < tokens, note, scale_ref[...])
     send_all(note_send, note_all, SC)
 
-    forward(2)
+    def ring_step(table, rings, step, kind):
+        arrive(rings[step - 1])
+        start(rings[step])
+        along_x(table.at[x, lax.rem(z + depth - step, depth)], kind)
+        along_x(table.at[x, lax.rem(z + step, depth)], kind)
+
+    def ring_end(table, rings, kind):
+        arrive(rings[-1])
+        along_x(table.at[x, lax.rem(z + depth // 2, depth)], kind)
+
+    ring_step(tok_all, token_rings, 1, (TX, TB))
+    send_part(down_hbm, down_mid, D1, portion, 2 * portion)
+    ring_step(tok_all, token_rings, 2, (TX, TB))
+    send_part(down_hbm, down_mid, D1, 2 * portion, 3 * portion)
+    ring_step(tok_all, token_rings, 3, (TX, TB))
+    send_part(down_hbm, down_mid, D1, 3 * portion, number)
+    pltpu.make_async_copy(down_hbm.at[e], down_mid.at[e], local_sem.at[D1]).start()
+
     load_first.wait()
     first_send[...] = grad_ref[...].astype(BF).reshape(first_send.shape)
     load_second.start()
 
-    sent_all(tok_recv, T)
-    send_all(down_hbm, down_mid, D1)
-
-    hit_slots = slot_hits(rank_after)
-    rest = weight_after
-    for p in range(3):
-        piece = rest.astype(BF)
-        rest = rest - piece.astype(F32)
-        wide = jnp.dot(spread, piece, preferred_element_type=F32)
-        pick_ref[p] = jnp.where(hit_slots, wide, 0.0).astype(BF)
-    forward(3, tokens // 2)
+    ring_end(tok_all, token_rings, (TX, TB))
+    small[3].wait()
+    start(cot_rings[0])
+    send_all(first_send, first_mid, F1)
+
+    load_gate.wait()
+    load_up.wait()
+    small[6].wait()
+    small[7].wait()
+
+    def dequantize(r, carry):
+        lines = pl.ds(pl.multiple_of(r * QB, QB), QB)
+        gate = (gate_v[lines, :].astype(F32) * gate_scale_ref[r]).astype(BF)
+        up = (up_v[lines, :].astype(F32) * up_scale_ref[r]).astype(BF)
+        weights_all[core, lines, :] = jnp.concatenate([gate, up], axis=1)
+        return carry
+
+    lax.fori_loop(0, gate_v.shape[0] // QB, dequantize, 0)
+    weights_copy = remote(weights_all.at[core], weights_all.at[core], W, sibling)
+    weights_copy.start()
+
+    def find(h, carry):
+        giver = jnp.int32(0)
+        for g in range(number):
+            giver = jnp.where(holder_ref[g] == h, g, giver)
+        giver_ref[h] = giver
+        return carry
+
+    lax.fori_loop(0, number, find, 0)
+
+    token_passed = pass_on(tok_all, (TX, TB), TF)
+    wait_all(note_send, note_all, SC)
+    for copy in token_passed:
+        copy.wait_recv()
+    slot = lax.broadcasted_iota(jnp.int32, (slots, tokens), 0).astype(F32)
+    for s in range(number):
+        hit = (note_all[s, 2:3, :tokens] == slot).astype(BF)
+        block = tok_all[s % columns, s // columns]
+        tok_recv[s] = jnp.dot(hit, block, preferred_element_type=F32).astype(BF)
+
+    up_chip = lax.rem(chip + 1, chips) * cores
+    down_chip = lax.rem(chip + chips - 1, chips) * cores
+    for c in range(cores):
+        src = tok_recv.at[pl.ds(c * half, half)]
+        remote(src, rows_all.at[d], YU + core, (e, up_chip + c)).start()
+        remote(src, rows_all.at[d], YD + core, (e, down_chip + c)).start()
+    rows_sibling = remote(
+        tok_recv.at[pl.ds((1 - core) * half, half)], rows_all.at[d], YS, sibling
+    )
+    rows_sibling.start()
+
     load_second.wait()
     second_send[...] = grad_ref[...].astype(BF).reshape(second_send.shape)
-
-    wait_all(tok_send, tok_recv, T)
-
-    def send_rows(k, carry):
-        t = lax.rem(d + k, parts)
-        src = tok_recv.at[pl.ds(lax.rem(t, cores) * half, half)]
-        remote(src, rows_all.at[d], Y1, (e, t)).start()
-        return carry
-
-    lax.fori_loop(1, parts, send_rows, 0)
-    own_rows = pltpu.make_async_copy(
-        tok_recv.at[pl.ds(core * half, half)], rows_all.at[d], local_sem.at[Y1]
-    )
-    own_rows.start()
-    for copy in rings[3]:
-        copy.wait_recv()
-
-    def send_column(k, carry):
-        t = (z * columns + lax.rem(x + k, columns), d)
-        remote(cot_all.at[x], cot_all.at[x], CX, t).start()
-        return carry
-
-    lax.fori_loop(1, columns, send_column, 0)
-    send_all(first_send, first_mid, F1)
+    arrive(cot_rings[0])
+    start(cot_rings[1])
     send_all(second_send, second_mid, S1)
-
     wait_all(down_hbm, down_mid, D1)
     reorder(down_mid, down_out)
     send_all(down_out, down_new, D2)
 
-    own_rows.wait()
+    def row_chunk(k):
+        return rows_all.at[k]
+
+    def arrived(kind, k):
+        remote(row_chunk(k), row_chunk(k), kind, sibling).wait_recv()
+
+    arrived(YU, down_chip)
+    pass_up = remote(row_chunk(down_chip), row_chunk(down_chip), YFU, (e, up_chip + core))
+    pass_up.start()
+    arrived(YD + 1, up_chip + 1)
+    pass_down = remote(
+        row_chunk(up_chip + 1), row_chunk(up_chip + 1), YFD, (e, down_chip + core)
+    )
+    pass_down.start()
+    arrive(cot_rings[1])
+    start(cot_rings[2])
+    wait_all(first_send, first_mid, F1)
+    reorder(first_mid, first_out)
+    send_all(first_out, first_new, F2)
+    arrive(cot_rings[2])
+    start(cot_rings[3])
+
+    rows_sibling.wait_recv()
     weights_copy.wait()
-    others = rows_all.at[pl.ds(0, parts - 1)]
-    remote(others, others, Y1, sibling).wait()
-    for c in range(cores):
-        value = jnp.zeros((half_rows, 2 * hidden_part), F32)
-        for k in range(parts):
-            value += jnp.dot(
-                rows_all[k].reshape(half_rows, width),
-                weights_all[c, k * width : (k + 1) * width, :],
-                preferred_element_type=F32,
-            )
+    arrived(YU + 1, down_chip + 1)
+    arrived(YD, up_chip)
+    far_chip = lax.rem(chip + 2, chips) * cores
+
+    def partial(chunk, values):
+        lines = pl.ds(pl.multiple_of(chunk * width, width), width)
+        return [
+            value
+            + jnp.dot(chunk_rows, weights_all[c, lines, :], preferred_element_type=F32)
+            for c, value in enumerate(values)
+        ]
+
+    values = [jnp.zeros((half_rows, 2 * hidden_part), F32) for _ in range(cores)]
+    own = tok_recv[pl.ds(core * half, half)].reshape(half_rows, width)
+    for chunk in (
+        d,
+        d + 1 - 2 * core,
+        down_chip,
+        down_chip + 1,
+        up_chip,
+        up_chip + 1,
+        far_chip,
+        far_chip + 1,
+    ):
+        if chunk is d:
+            chunk_rows = own
+        else:
+            if chunk is far_chip:
+                arrived(YFU, far_chip)
+                arrived(YFD, far_chip + 1)
+            chunk_rows = rows_all[chunk].reshape(half_rows, width)
+        values = partial(chunk, values)
+    for c, value in enumerate(values):
         gate = value[:, :hidden_part]
         up = value[:, hidden_part:]
         act = (gate / (1.0 + jnp.exp(-gate)) * up).astype(BF)
@@ -368,42 +445,67 @@
             number, half_rows // number, hidden_part
         )
     send_all(hid_send, hid_mid, H1)
-
-    wait_all(first_send, first_mid, F1)
-    reorder(first_mid, first_out)
-    send_all(first_out, first_new, F2)
+    arrive(cot_rings[-1])
+    along_x(cot_all.at[x], (CX, CB))
+
 
     wait_all(hid_send, hid_mid, H1)
     reorder(hid_mid, hid_out)
     send_all(hid_out, hid_new, H2)
-
     wait_all(second_send, second_mid, S1)
     reorder(second_mid, second_out)
     send_all(second_out, second_new, S2)
 
+
+    row = lax.broadcasted_iota(jnp.int32, (total, number), 0)
+    holder = lax.broadcasted_iota(jnp.int32, (total, number), 1)
+    spread = jnp.logical_and(row >= holder * slots, row < (holder + 1) * slots).astype(BF)
+    place = lax.rem(lax.broadcasted_iota(jnp.int32, (total, tokens), 0), slots).astype(F32)
+    wide_rank = jnp.dot(
+        spread, lanes_ref[0, :, :tokens].astype(BF), preferred_element_type=F32
+    )
+    hit_slots = wide_rank == place
+    rest = lanes_ref[1, :, :tokens]
+    for p in range(pick_ref.shape[0]):
+        piece = rest.astype(BF)
+        rest = rest - piece.astype(F32)
+        wide = jnp.dot(spread, piece, preferred_element_type=F32)
+        pick_ref[p] = jnp.where(hit_slots, wide, 0.0).astype(BF)
+    save_pick = pltpu.make_async_copy(pick_ref, pick_hbm, load_sem.at[1])
+    save_pick.start()
+
     wait_all(hid_out, hid_new, H2)
 
-    def send_hidden(k, carry):
-        remote(hid_new, hidden_all.at[d], Y2, (e, lax.rem(d + k, parts))).start()
-        return carry
-
-    lax.fori_loop(1, parts, send_hidden, 0)
     own_hidden = pltpu.make_async_copy(hid_new, hidden_all.at[d], local_sem.at[Y2])
     own_hidden.start()
-
-    wait_all(note_send, note_all, SC)
+    for k in range(1, chips):
+        target = lax.rem(chip + k, chips) * cores + core
+        remote(hid_new, hidden_all.at[d], Y2, (e, target)).start()
+    remote(hid_new, hidden_all.at[d], Y3, sibling).start()
+
+    others = hidden_all.at[pl.ds(0, chips - 1)]
+    remote(others, others, Y2, sibling).wait_recv()
+    for k in range(1, chips):
+        chunk = hidden_all.at[lax.rem(chip + k, chips) * cores + core]
+        remote(chunk, chunk, Y3, sibling).start()
+
+    cot_passed = pass_on(cot_all, (CX, CB), CF)
     wait_all(down_out, down_new, D2)
     save_down = pltpu.make_async_copy(down_new, down_new_hbm, load_sem.at[0])
     save_down.start()
-    save_pick = pltpu.make_async_copy(pick_ref, pick_hbm, load_sem.at[1])
-    save_pick.start()
     scale = note_all[giver_ref[e]]
     scale_wide = jnp.concatenate(
         [
-            jnp.broadcast_to(scale[:, tokens + c : tokens + c + 1], (scale.shape[0], QB))
-            for c in range(width // QB)
+            jnp.concatenate(
+                [
+                    jnp.broadcast_to(scale[c : c + 1, tokens + r : tokens + r + 1], (1, QB))
+                    for c in range(width // QB)
+                ],
+                axis=1,
+            )
+            for r in range(wide_ref.shape[0])
         ],
-        axis=1,
+        axis=0,
     )
     wide_ref[...] = scale_wide
     save_wide = pltpu.make_async_copy(wide_ref, wide_hbm, load_sem.at[2])
@@ -415,12 +517,12 @@
         return (quant.astype(F32) * scale_wide[r : r + 1, :]).astype(BF)
 
     own_hidden.wait()
-    others = hidden_all.at[pl.ds(0, parts - 1)]
-    remote(others, others, Y2, sibling).wait()
+    others = hidden_all.at[pl.ds(0, chips)]
+    remote(others, others, Y3, sibling).wait_recv()
     pair = cores * hidden_part
     for c in range(cores):
         value = jnp.zeros((half_rows, width), F32)
-        for y in range(parts // cores):
+        for y in range(chips):
             down_w = jnp.concatenate(
                 [weight_rows(y * pair // QB + r) for r in range(pair // QB)], axis=0
             )
@@ -432,17 +534,15 @@
         out_send[c * half : (c + 1) * half] = value.astype(BF).reshape(half, slots, width)
     send_all(out_send, out_recv, O)
 
-    others = cot_all.at[pl.ds(0, columns - 1)]
-    remote(others, others, CX, sibling).wait()
+    for copy in cot_passed:
+        copy.wait_recv()
     for s in range(number):
-        slot = lax.broadcasted_iota(jnp.int32, (slots, tokens), 0).astype(F32)
         hit = note_all[s, 0:1, :tokens] == slot
         weight = jnp.sum(jnp.where(hit, note_all[s, 1:2, :tokens], 0.0), axis=1, keepdims=True)
         block = cot_all[s % columns, s // columns]
         picked = jnp.dot(hit.astype(BF), block, preferred_element_type=F32)
         back_ref[s] = (weight * picked).astype(BF)
-
-    for y in range(parts // cores):
+    for y in range(chips):
         value = jnp.zeros((pair, width), F32)
         for c in range(cores):
             value += transposed_dot(
@@ -453,9 +553,24 @@
     save_grad = pltpu.make_async_copy(grad_ref, grad_hbm, load_sem.at[3])
     save_grad.start()
 
-    for pair_of_copies in rings:
-        for copy in pair_of_copies:
+    for copies in token_rings + cot_rings:
+        for copy in copies:
             copy.wait_send()
+    for table, kinds in ((tok_all, (TX, TB)), (cot_all, (CX, CB))):
+        for kind in kinds:
+            remote(table.at[0], table.at[0], kind, sibling).wait_send()
+    for copy in token_passed + cot_passed:
+        copy.wait_send()
+    both = rows_all.at[pl.ds(0, cores)]
+    remote(both, both, YU + core, sibling).wait_send()
+    remote(both, both, YD + core, sibling).wait_send()
+    rows_sibling.wait_send()
+    pass_up.wait_send()
+    pass_down.wait_send()
+    others = hidden_all.at[pl.ds(0, chips - 1)]
+    remote(others, others, Y2, sibling).wait_send()
+    others = hidden_all.at[pl.ds(0, chips)]
+    remote(others, others, Y3, sibling).wait_send()
     for dst, kind in (
         (note_all, SC),
         (down_mid, D1),
@@ -497,7 +612,6 @@
         rows = rows_ref[...].reshape(-1, width)
         value = transposed_dot(pick_ref[0], rows)
         value += transposed_dot(pick_ref[1], rows)
-        value += transposed_dot(pick_ref[2], rows)
         mixed_ref[...] = value.astype(BF)
 
     grad = grad_ref[...]
@@ -524,7 +638,7 @@
     hidden_total, width = grad.shape
     number, piece_rows, _ = down_new.shape
     tokens = pick.shape[2]
-    steps = 4
+    steps = 2
     tall = hidden_total // steps
     state = pl.BlockSpec((number // steps, piece_rows, width), lambda k: (k, 0, 0))
     block = pl.BlockSpec((1, tall, width), lambda k: (0, k, 0))
@@ -578,14 +692,15 @@
     model_width, hidden_part = gate_quant.shape[1:]
     hidden_total = down_quant.shape[1]
     piece_rows = hidden_total // number
-    scale_cols = down_scale.shape[2]
-    scale = jnp.pad(down_scale[0], ((0, 0), (tok_rows, QB - tok_rows - scale_cols)))
+    scale = jnp.pad(
+        down_scale[0].T, ((0, 0), (tok_rows, QB - tok_rows - hidden_total // QB))
+    )
 
     hbm = pl.BlockSpec(memory_space=pl.ANY)
     state_shape = (number, piece_rows, width)
     row_shape = (number, slots, width)
-    pick_shape = (3, number * slots, tok_rows)
-    wide_shape = (scale.shape[0], width)
+    pick_shape = (2, number * slots, tok_rows)
+    wide_shape = (hidden_total // QB, width)
     half_rows = number * slots // cores
     state = pltpu.VMEM(state_shape, BF)
     rows = pltpu.VMEM(row_shape, BF)
@@ -612,11 +727,10 @@
             pltpu.SMEM((model_width // QB,), F32),
             pltpu.VMEM((top_count, tok_rows), jnp.int32),
             pltpu.VMEM((top_count, tok_rows), F32),
-            pltpu.VMEM((tok_rows, width), BF),
             pltpu.VMEM(scale.shape, F32),
             pltpu.SMEM((number,), jnp.int32),
-            pltpu.VMEM((2, number, QB), F32),
-            rows,
+            pltpu.VMEM((3, number, QB), F32),
+            pltpu.VMEM((columns, number // columns, tok_rows, width), BF),
             rows,
             note,
             note,

time: 234 us -> 224 us (0.957)
  Pallas kernels: 232 us -> 220 us
    pallas_call x1, Pallas kernels: 224 us -> 213 us  [per_device(): pl.pallas_call(step_kernel, in_specs=[hbm] * 14, out_specs=[hbm] * 7, out...]
where the time goes in v4:
time: 224 us; the launch traced here: 222 us
  Pallas kernels  220 us (98%)
    pallas_call x1, Pallas kernels, per_device(): pl.pallas_call(step_kernel, in_specs=[hbm] * 14, out_specs=[hbm] * 7, out...  213 us
    pallas_call x1, Pallas kernels, finish(): pl.pallas_call(finish_kernel, grid=(steps,), in_specs=[pl.BlockSpec((tall...  6.31 us

profile of v4, /device:TPU:1, one launch (start us, length us, event | category | flops | bytes accessed | tf_op | source)
XLA Modules:
  0.0 221.5 jit_solution(11022670806076861858)
XLA Ops:
  0.6 1.3 pad.4.scale_hbm
  2.0 213.3 %step.1 = (f32[1024,512]{1,0:T(8,128)}, bf16[32,32,512]{2,1,0:T(8,128)(2,1)}, bf16[32,32,512]{2,1,0:T(8,128)(2,1)}, bf16[32,32,512]{2,1,0:T(8,128)(2,1)}, bf16[3...) custom-call(s32[32]{0:T(128)} %old_hbm.1, s32[32]{0:T(128)} %holder_hbm.1, f32[32]{0:T(128)} %bitcast.20, ...), custom_call_target="tpu_custom_call" | custom-call | tf_op jit(solution)/shard_map/step/pallas_call | solution.py:710
  215.2 6.3 %finish.1 = (bf16[96,512]{1,0:T(8,128)(2,1)}, bf16[1,1024,512]{2,1,0:T(8,128)(2,1)}, f32[1,1024,512]{2,1,0:T(8,128)}, f32[1,1024,512]{2,1,0:T(8,128)}) custom-call(f32[1024,512]{1,0:T(8,128)} %get-tuple-element.11.grad_ref, bf16[32,32,512]{2,1,0:T(8,128)(2,1)} %get-tuple-element.12.down_ref, bf16[32,32,512]{2,1,0:T(8,128)(2,1)} %get-tuple-element.13.first_in, ...), custom_call_target="tpu_custom_call" | custom-call | tf_op jit(solution)/shard_map/finish/pallas_call | solution.py:645

commit v5 on v4

--- a/solution.py
+++ b/solution.py
@@ -66,6 +66,7 @@
     route_ref,
     weight_ref,
     scale_ref,
+    scale_lanes,
     giver_ref,
     lanes_ref,
     tok_all,
@@ -288,6 +289,9 @@
     lanes_ref[0, :, :tokens] = rank_after
     lanes_ref[1, :, :tokens] = weight_after
     lanes_ref[2, :, :tokens] = ranks(hit_before)
+    scale_lanes[...] = jnp.zeros_like(scale_lanes)
+    scale_lanes[: scale_ref.shape[0], : scale_ref.shape[1]] = scale_ref[...]
+    scale_note = pltpu.roll(scale_lanes[...], tokens, 1)[: scale_ref.shape[0], :]
     note_shape = note_send.shape[1:]
     line = lax.broadcasted_iota(jnp.int32, note_shape, 0)
     lane = lax.broadcasted_iota(jnp.int32, note_shape, 1)
@@ -296,7 +300,7 @@
         for r in range(3):
             spread_row = jnp.broadcast_to(lanes_ref[r, h : h + 1, :], note_shape)
             note = jnp.where(line == r, spread_row, note)
-        note_send[h] = jnp.where(lane < tokens, note, scale_ref[...])
+        note_send[h] = jnp.where(lane < tokens, note, scale_note)
     send_all(note_send, note_all, SC)
 
     def ring_step(table, rings, step, kind):
@@ -397,9 +401,6 @@
     pass_down.start()
     arrive(cot_rings[1])
     start(cot_rings[2])
-    wait_all(first_send, first_mid, F1)
-    reorder(first_mid, first_out)
-    send_all(first_out, first_new, F2)
     arrive(cot_rings[2])
     start(cot_rings[3])
 
@@ -445,6 +446,9 @@
             number, half_rows // number, hidden_part
         )
     send_all(hid_send, hid_mid, H1)
+    wait_all(first_send, first_mid, F1)
+    reorder(first_mid, first_out)
+    send_part(first_out, first_new, F2, 1, number // 2)
     arrive(cot_rings[-1])
     along_x(cot_all.at[x], (CX, CB))
 
@@ -452,6 +456,8 @@
     wait_all(hid_send, hid_mid, H1)
     reorder(hid_mid, hid_out)
     send_all(hid_out, hid_new, H2)
+    send_part(first_out, first_new, F2, number // 2, number)
+    pltpu.make_async_copy(first_out.at[e], first_new.at[e], local_sem.at[F2]).start()
     wait_all(second_send, second_mid, S1)
     reorder(second_mid, second_out)
     send_all(second_out, second_new, S2)
@@ -592,10 +598,19 @@
 
 
 def finish_kernel(
+    grad_hbm,
+    down_hbm,
+    first_hbm,
+    second_hbm,
+    wide_hbm,
+    pick_hbm,
+    rows_hbm,
+    mixed_hbm,
+    fresh_hbm,
+    first_out,
+    second_out,
     grad_ref,
-    down_ref,
-    first_in,
-    second_in,
+    state_ref,
     wide_ref,
     pick_ref,
     rows_ref,
@@ -603,63 +618,103 @@
     fresh_ref,
     first_ref,
     second_ref,
+    load_sem,
+    store_sem,
+    other_sem,
 ):
-    k = pl.program_id(0)
-    tall, width = grad_ref.shape
-
-    @pl.when(k == 0)
-    def _():
-        rows = rows_ref[...].reshape(-1, width)
-        value = transposed_dot(pick_ref[0], rows)
-        value += transposed_dot(pick_ref[1], rows)
-        mixed_ref[...] = value.astype(BF)
-
-    grad = grad_ref[...]
-    quant = down_ref[...].reshape(tall, width).astype(F32)
-    lines = tall // QB
-    master = jnp.concatenate(
-        [
-            quant[r * QB : (r + 1) * QB, :] * wide_ref[pl.ds(k * lines + r, 1), :]
-            for r in range(lines)
-        ],
-        axis=0,
-    )
-    first = first_in[...].reshape(tall, width).astype(F32)
-    second = second_in[...].reshape(tall, width).astype(F32)
-    first = beta_first * first + (1.0 - beta_first) * grad
-    second = beta_second * second + (1.0 - beta_second) * grad * grad
-    update = first / fix_first / (jnp.sqrt(second / fix_second) + adam_eps)
-    fresh_ref[0] = (master - learn_rate * (update + decay_rate * master)).astype(BF)
-    first_ref[0] = first
-    second_ref[0] = second
+    total, width = grad_ref.shape
+    tall = QB
+    chunks = total // tall
+    pieces = tall // state_ref.shape[2]
+    others = [
+        pltpu.make_async_copy(src, dst, other_sem.at[k])
+        for k, (src, dst) in enumerate(
+            [(wide_hbm, wide_ref), (pick_hbm, pick_ref), (rows_hbm, rows_ref)]
+        )
+    ]
+    others[0].start()
+    loads = []
+    for r in range(chunks):
+        rows = pl.ds(r * tall, tall)
+        block = pl.ds(r * pieces, pieces)
+        copies = [pltpu.make_async_copy(grad_hbm.at[rows], grad_ref.at[rows], load_sem.at[r, 0])]
+        for k, src in enumerate((down_hbm, first_hbm, second_hbm)):
+            copies.append(
+                pltpu.make_async_copy(
+                    src.at[block], state_ref.at[k, block], load_sem.at[r, k + 1]
+                )
+            )
+        for copy in copies:
+            copy.start()
+        loads.append(copies)
+    others[1].start()
+    others[2].start()
+    others[0].wait()
+    stores = []
+    for r in range(chunks):
+        for copy in loads[r]:
+            copy.wait()
+        rows = pl.ds(r * tall, tall)
+        block = pl.ds(r * pieces, pieces)
+        grad = grad_ref[rows, :]
+        quant = state_ref[0, block].reshape(tall, width).astype(F32)
+        master = quant * wide_ref[r : r + 1, :]
+        first = state_ref[1, block].reshape(tall, width).astype(F32)
+        second = state_ref[2, block].reshape(tall, width).astype(F32)
+        first = beta_first * first + (1.0 - beta_first) * grad
+        second = beta_second * second + (1.0 - beta_second) * grad * grad
+        size = jnp.sqrt(second * (1.0 / fix_second)) + adam_eps
+        update = first * (1.0 / fix_first) / size
+        first_ref[rows, :] = first
+        second_ref[rows, :] = second
+        fresh_ref[rows, :] = (master - learn_rate * (update + decay_rate * master)).astype(BF)
+        for k, (src, dst) in enumerate(
+            ((first_ref, first_out), (second_ref, second_out), (fresh_ref, fresh_hbm))
+        ):
+            store = pltpu.make_async_copy(src.at[rows], dst.at[0, rows], store_sem.at[r, k])
+            store.start()
+            stores.append(store)
+    others[1].wait()
+    others[2].wait()
+    returned = rows_ref[...].reshape(-1, width)
+    value = transposed_dot(pick_ref[0], returned)
+    value += transposed_dot(pick_ref[1], returned)
+    mixed_ref[...] = value.astype(BF)
+    store = pltpu.make_async_copy(mixed_ref, mixed_hbm, other_sem.at[3])
+    store.start()
+    stores.append(store)
+    for store in stores:
+        store.wait()
 
 
 def finish(grad, down_new, first_new, second_new, wide, pick, out_rows):
     hidden_total, width = grad.shape
-    number, piece_rows, _ = down_new.shape
     tokens = pick.shape[2]
-    steps = 2
-    tall = hidden_total // steps
-    state = pl.BlockSpec((number // steps, piece_rows, width), lambda k: (k, 0, 0))
-    block = pl.BlockSpec((1, tall, width), lambda k: (0, k, 0))
+    chunks = hidden_total // QB
+    hbm = pl.BlockSpec(memory_space=pl.ANY)
     return pl.pallas_call(
         finish_kernel,
-        grid=(steps,),
-        in_specs=[
-            pl.BlockSpec((tall, width), lambda k: (k, 0)),
-            state,
-            state,
-            state,
-            pl.BlockSpec(wide.shape, lambda k: (0, 0)),
-            pl.BlockSpec(pick.shape, lambda k: (0, 0, 0)),
-            pl.BlockSpec(out_rows.shape, lambda k: (0, 0, 0)),
-        ],
-        out_specs=[pl.BlockSpec((tokens, width), lambda k: (0, 0)), block, block, block],
+        in_specs=[hbm] * 7,
+        out_specs=[hbm] * 4,
         out_shape=[
             jax.ShapeDtypeStruct((tokens, width), BF),
             jax.ShapeDtypeStruct((1, hidden_total, width), BF),
             jax.ShapeDtypeStruct((1, hidden_total, width), F32),
             jax.ShapeDtypeStruct((1, hidden_total, width), F32),
+        ],
+        scratch_shapes=[
+            pltpu.VMEM((hidden_total, width), F32),
+            pltpu.VMEM((3,) + down_new.shape, BF),
+            pltpu.VMEM(wide.shape, F32),
+            pltpu.VMEM(pick.shape, BF),
+            pltpu.VMEM(out_rows.shape, BF),
+            pltpu.VMEM((tokens, width), BF),
+            pltpu.VMEM((hidden_total, width), BF),
+            pltpu.VMEM((hidden_total, width), F32),
+            pltpu.VMEM((hidden_total, width), F32),
+            pltpu.SemaphoreType.DMA((chunks, 4)),
+            pltpu.SemaphoreType.DMA((chunks, 3)),
+            pltpu.SemaphoreType.DMA((4,)),
         ],
         compiler_params=pltpu.CompilerParams(vmem_limit_bytes=VMEM_LIMIT),
         name="finish",
@@ -692,9 +747,7 @@
     model_width, hidden_part = gate_quant.shape[1:]
     hidden_total = down_quant.shape[1]
     piece_rows = hidden_total // number
-    scale = jnp.pad(
-        down_scale[0].T, ((0, 0), (tok_rows, QB - tok_rows - hidden_total // QB))
-    )
+    scale = down_scale[0].T
 
     hbm = pl.BlockSpec(memory_space=pl.ANY)
     state_shape = (number, piece_rows, width)
@@ -704,7 +757,7 @@
     half_rows = number * slots // cores
     state = pltpu.VMEM(state_shape, BF)
     rows = pltpu.VMEM(row_shape, BF)
-    note = pltpu.VMEM((number,) + scale.shape, F32)
+    note = pltpu.VMEM((number, scale.shape[0], QB), F32)
     hid_shape = (number, half_rows // number, cores * hidden_part)
     hid = pltpu.VMEM(hid_shape, BF)
     parts_out = pl.pallas_call(
@@ -728,6 +781,7 @@
             pltpu.VMEM((top_count, tok_rows), jnp.int32),
             pltpu.VMEM((top_count, tok_rows), F32),
             pltpu.VMEM(scale.shape, F32),
+            pltpu.VMEM((8, QB), F32),
             pltpu.SMEM((number,), jnp.int32),
             pltpu.VMEM((3, number, QB), F32),
             pltpu.VMEM((columns, number // columns, tok_rows, width), BF),

time: 224 us -> 214 us (0.955)
  Pallas kernels: 220 us -> 211 us
    pallas_call x1, Pallas kernels: 213 us -> 204 us  [per_device(): pl.pallas_call(step_kernel, in_specs=[hbm] * 14, out_specs=[hbm] * 7, out...]
where the time goes in v5:
time: 214 us; the launch traced here: 211 us
  Pallas kernels  211 us (99%)
    pallas_call x1, Pallas kernels, per_device(): pl.pallas_call(step_kernel, in_specs=[hbm] * 14, out_specs=[hbm] * 7, out...  204 us
    pallas_call x1, Pallas kernels, finish(): pl.pallas_call(finish_kernel, in_specs=[hbm] * 7, out_specs=[hbm] * 4, ou...  6.32 us

profile of v5, /device:TPU:1, one launch (start us, length us, event | category | flops | bytes accessed | tf_op | source)
XLA Modules:
  0.0 211.4 jit_solution(144808384385412793)
XLA Ops:
  0.6 204.5 %step.1 = (f32[1024,512]{1,0:T(8,128)}, bf16[32,32,512]{2,1,0:T(8,128)(2,1)}, bf16[32,32,512]{2,1,0:T(8,128)(2,1)}, bf16[32,32,512]{2,1,0:T(8,128)(2,1)}, bf16[3...) custom-call(s32[32]{0:T(128)} %old_hbm.1, s32[32]{0:T(128)} %holder_hbm.1, f32[32]{0:T(128)} %bitcast.20, ...), custom_call_target="tpu_custom_call" | custom-call | tf_op jit(solution)/shard_map/step/pallas_call | solution.py:763
  205.1 6.3 %finish.1 = (bf16[96,512]{1,0:T(8,128)(2,1)}, bf16[1,1024,512]{2,1,0:T(8,128)(2,1)}, f32[1,1024,512]{2,1,0:T(8,128)}, f32[1,1024,512]{2,1,0:T(8,128)}) custom-call(f32[1024,512]{1,0:T(8,128)} %get-tuple-element.11.grad_hbm, bf16[32,32,512]{2,1,0:T(8,128)(2,1)} %get-tuple-element.12.down_hbm, bf16[32,32,512]{2,1,0:T(8,128)(2,1)} %get-tuple-element.13.first_hbm, ...), custom_call_target="tpu_custom_call" | custom-call | tf_op jit(solution)/shard_map/finish/pallas_call | solution.py:695

commit v6 on v5

--- a/solution.py
+++ b/solution.py
@@ -538,7 +538,18 @@
                 preferred_element_type=F32,
             )
         out_send[c * half : (c + 1) * half] = value.astype(BF).reshape(half, slots, width)
-    send_all(out_send, out_recv, O)
+
+        def send_half(k, carry, c=c):
+            t = c * half + lax.rem(e + k, half)
+
+            @pl.when(t != e)
+            def _():
+                remote(out_send.at[t], out_recv.at[e], O, (t, d)).start()
+
+            return carry
+
+        lax.fori_loop(0, half, send_half, 0)
+    pltpu.make_async_copy(out_send.at[e], out_recv.at[e], local_sem.at[O]).start()
 
     for copy in cot_passed:
         copy.wait_recv()
@@ -623,7 +634,7 @@
     other_sem,
 ):
     total, width = grad_ref.shape
-    tall = QB
+    tall = 2 * QB
     chunks = total // tall
     pieces = tall // state_ref.shape[2]
     others = [
@@ -658,7 +669,13 @@
         block = pl.ds(r * pieces, pieces)
         grad = grad_ref[rows, :]
         quant = state_ref[0, block].reshape(tall, width).astype(F32)
-        master = quant * wide_ref[r : r + 1, :]
+        master = jnp.concatenate(
+            [
+                quant[:QB, :] * wide_ref[2 * r : 2 * r + 1, :],
+                quant[QB:, :] * wide_ref[2 * r + 1 : 2 * r + 2, :],
+            ],
+            axis=0,
+        )
         first = state_ref[1, block].reshape(tall, width).astype(F32)
         second = state_ref[2, block].reshape(tall, width).astype(F32)
         first = beta_first * first + (1.0 - beta_first) * grad
@@ -690,7 +707,7 @@
 def finish(grad, down_new, first_new, second_new, wide, pick, out_rows):
     hidden_total, width = grad.shape
     tokens = pick.shape[2]
-    chunks = hidden_total // QB
+    chunks = hidden_total // (2 * QB)
     hbm = pl.BlockSpec(memory_space=pl.ANY)
     return pl.pallas_call(
         finish_kernel,

time: 214 us -> 215 us (level)
  the two profiles are of different devices: /device:TPU:1 before, /device:TPU:32 now
where the time goes in v6:
time: 215 us; the launch traced here: 214 us
  Pallas kernels  214 us (100%)
    pallas_call x1, Pallas kernels, per_device(): pl.pallas_call(step_kernel, in_specs=[hbm] * 14, out_specs=[hbm] * 7, out...  208 us
    pallas_call x1, Pallas kernels, finish(): pl.pallas_call(finish_kernel, in_specs=[hbm] * 7, out_specs=[hbm] * 4, ou...  5.9 us

profile of v6, /device:TPU:32, one launch (start us, length us, event | category | flops | bytes accessed | tf_op | source)
XLA Modules:
  0.0 214.5 jit_solution(18097873247375268949)
XLA Ops:
  0.6 207.9 %step.1 = (f32[1024,512]{1,0:T(8,128)}, bf16[32,32,512]{2,1,0:T(8,128)(2,1)}, bf16[32,32,512]{2,1,0:T(8,128)(2,1)}, bf16[32,32,512]{2,1,0:T(8,128)(2,1)}, bf16[3...) custom-call(s32[32]{0:T(128)} %old_hbm.1, s32[32]{0:T(128)} %holder_hbm.1, f32[32]{0:T(128)} %bitcast.20, ...), custom_call_target="tpu_custom_call" | custom-call | tf_op jit(solution)/shard_map/step/pallas_call | solution.py:780
  208.6 5.9 %finish.1 = (bf16[96,512]{1,0:T(8,128)(2,1)}, bf16[1,1024,512]{2,1,0:T(8,128)(2,1)}, f32[1,1024,512]{2,1,0:T(8,128)}, f32[1,1024,512]{2,1,0:T(8,128)}) custom-call(f32[1024,512]{1,0:T(8,128)} %get-tuple-element.11.grad_hbm, bf16[32,32,512]{2,1,0:T(8,128)(2,1)} %get-tuple-element.12.down_hbm, bf16[32,32,512]{2,1,0:T(8,128)(2,1)} %get-tuple-element.13.first_hbm, ...), custom_call_target="tpu_custom_call" | custom-call | tf_op jit(solution)/shard_map/finish/pallas_call | solution.py:712
